TPU v7x, 32 devices: a whole 2x2x4 slice. The times are simulated.
32 devices in a mesh: dp: 16 (over z, y, x), seq: 2 (over core).
Axes of the slice: x: 2, y: 2, z: 4, core: 2. Of those that a mesh axis runs over, the one named last changes fastest.
Arguments:
- tokens: bfloat16 [64, 512, 768], P('dp', 'seq'), may hold values from -6 to 6
- cotangent: bfloat16 [64, 512, 768], P('dp', 'seq'), may hold values from -6 to 6
- seq_lengths: int32 [16, 4], P('dp'), may hold values from 1 to 512, 1536 in all within a row
- slot_order: int32 [16, 4], P('dp'), may hold values from 0 to 3, each once within a row
- attn_weights: float32 [768, 3072], P(None, ('dp', 'seq'))
- attn_moment: float32 [768, 3072], P(None, ('dp', 'seq'))
- attn_second: float32 [768, 3072], P(None, ('dp', 'seq')), as said below
- ffn_weights: float32 [768, 6144], P(None, ('dp', 'seq'))
- ffn_moment: float32 [768, 6144], P(None, ('dp', 'seq'))
- ffn_second: float32 [768, 6144], P(None, ('dp', 'seq')), as said below
- vectors: float32 [9216], P(('dp', 'seq'))
- vector_moment: float32 [9216], P(('dp', 'seq'))
- vector_second: float32 [9216], P(('dp', 'seq')), as said below
Outputs:
- layer_out: bfloat16 [64, 512, 768], P('dp', 'seq')
- input_grad: float32 [64, 512, 768], P('dp', 'seq')
- attn_moment_out: float32 [768, 3072], P(None, ('dp', 'seq'))
- attn_second_out: float32 [768, 3072], P(None, ('dp', 'seq'))
- attn_weights_out: float32 [768, 3072], P(None, ('dp', 'seq'))
- attn_copy_out: bfloat16 [768, 3072], P(None, ('dp', 'seq'))
- ffn_moment_out: float32 [768, 6144], P(None, ('dp', 'seq'))
- ffn_second_out: float32 [768, 6144], P(None, ('dp', 'seq'))
- ffn_weights_out: float32 [768, 6144], P(None, ('dp', 'seq'))
- ffn_copy_out: bfloat16 [768, 6144], P(None, ('dp', 'seq'))
- vector_moment_out: float32 [9216], P(('dp', 'seq'))
- vector_second_out: float32 [9216], P(('dp', 'seq'))
- vectors_out: float32 [9216], P(('dp', 'seq'))
- vector_copy_out: bfloat16 [9216], P(('dp', 'seq'))
Inputs may be any that keep to these rules, and one draw needn't show every extreme that they name: `seq_lengths`: in each group the 4 lengths sum to 1536 and the largest is exactly 512. `slot_order`: each group's row is a permutation of 0 to 3. `attn_second`: Positive. `ffn_second`: Positive. `vector_second`: Positive.
All inputs are finite; a program needn't handle non-finite values.
Results may differ from a plain program's by a relative error of at most 0.012.
The roundings to bfloat16 on the way count: a program that leaves them out, or rounds other values in their place, can miss the bound.
Values may be sent and summed in bfloat16 or wider, within the bound.
No kernel may reach another device: no remote copies, remote signals or barrier semaphores. Data moves between devices by JAX's collectives and lax.ppermute only.
A program may use at most 192 MiB of HBM per device.

v0:
```python
import math

import jax
import jax.numpy as jnp
from jax import lax
from jax.sharding import PartitionSpec as P

H = 12
FF = 3072
STEP = 5


epsilon = 1e-06
masked_score = -1e30
decay_rate = 0.5
adam_epsilon = 1e-08
weight_decay = 0.01
vector_rate = 0.5


def norm_forward(values, gain_vec, shift_vec):
    center = values - jnp.mean(values, axis=-1, keepdims=True)
    inverse = lax.rsqrt(jnp.mean(center * center, axis=-1, keepdims=True) + epsilon)
    normed = center * inverse
    return (normed * gain_vec + shift_vec, normed, inverse)


def norm_backward(upstream, normed, inverse, gain_vec):
    scaled_grad = upstream * gain_vec
    centered = scaled_grad - jnp.mean(scaled_grad, axis=-1, keepdims=True)
    return inverse * (centered - normed * jnp.mean(scaled_grad * normed, axis=-1, keepdims=True))


def contract_rows(left, right):
    return lax.dot_general(
        left, right, (((0,), (0,)), ((), ())), preferred_element_type=jnp.float32
    )


def contract_cols(left, right):
    return lax.dot_general(
        left, right, (((1,), (1,)), ((), ())), preferred_element_type=jnp.float32
    )


def gelu_exact(values):
    return jax.nn.gelu(values, approximate=False)


def attend_forward(packed):
    query_blk, key_blk, value_blk, live_mask = packed
    scores = jnp.einsum("qhd,khd->hqk", query_blk, key_blk, preferred_element_type=jnp.float32)
    scores = jnp.where(live_mask[None, None, :], scores, masked_score)
    row_max = jnp.max(scores, axis=-1, keepdims=True)
    exp_terms = jnp.exp(scores - row_max)
    totals = jnp.sum(exp_terms, axis=-1, keepdims=True)
    probs = exp_terms / totals
    log_total = row_max + jnp.log(totals)
    context_rows = jnp.einsum(
        "hqk,khd->qhd", probs.astype(jnp.bfloat16), value_blk, preferred_element_type=jnp.float32
    )
    return (context_rows.astype(jnp.bfloat16), log_total)


def attend_backward(packed):
    query_blk, key_blk, value_blk, live_mask, log_total, grad_ctx = packed
    scores = jnp.einsum("qhd,khd->hqk", query_blk, key_blk, preferred_element_type=jnp.float32)
    scores = jnp.where(live_mask[None, None, :], scores, masked_score)
    probs = jnp.exp(scores - log_total)
    grad_prob = jnp.einsum("qhd,khd->hqk", grad_ctx, value_blk, preferred_element_type=jnp.float32)
    grad_value = jnp.einsum(
        "hqk,qhd->khd", probs.astype(jnp.bfloat16), grad_ctx, preferred_element_type=jnp.float32
    )
    inner = jnp.sum(probs * grad_prob, axis=-1, keepdims=True)
    grad_score = (probs * (grad_prob - inner)).astype(jnp.bfloat16)
    grad_query = jnp.einsum("hqk,khd->qhd", grad_score, key_blk, preferred_element_type=jnp.float32)
    grad_key = jnp.einsum("hqk,qhd->khd", grad_score, query_blk, preferred_element_type=jnp.float32)
    length = query_blk.shape[0]
    stacked = jnp.stack(
        [
            grad_query.reshape(length, -1),
            grad_key.reshape(length, -1),
            grad_value.reshape(length, -1),
        ],
        axis=1,
    )
    return stacked.astype(jnp.bfloat16)


def adam_update(master, moment, second, grad, rate):
    moment_new = decay_rate * moment + (1.0 - decay_rate) * grad
    second_new = decay_rate * second + (1.0 - decay_rate) * grad * grad
    correction = 1.0 - decay_rate**STEP
    direction = moment_new / correction / (jnp.sqrt(second_new / correction) + adam_epsilon)
    master_new = master - rate * (direction + weight_decay * master)
    return (moment_new, second_new, master_new)


def local(
    tokens,
    cotangent,
    seq_lengths,
    slot_order,
    attn_weights,
    attn_moment,
    attn_second,
    ffn_weights,
    ffn_moment,
    ffn_second,
    vectors,
    vector_moment,
    vector_second,
):
    seq_parts = lax.axis_size("seq")
    seq_count, half_len, width = tokens.shape
    full_len = half_len * seq_parts
    head_dim = width // H
    heads_here = H // seq_parts
    head_width = width // seq_parts
    tok_rows = seq_count * half_len
    slot_pick = (slot_order[0][:, None] == jnp.arange(seq_count)[None, :]).astype(jnp.int32)
    slot_len = jnp.sum(slot_pick * seq_lengths[0][None, :], axis=1)
    attn_used, ffn_used, vec_used = (
        lax.all_gather(attn_weights.astype(jnp.bfloat16), ("dp", "seq"), axis=1, tiled=True),
        lax.all_gather(ffn_weights.astype(jnp.bfloat16), ("dp", "seq"), axis=1, tiled=True),
        lax.all_gather(vectors.astype(jnp.bfloat16), ("dp", "seq"), axis=0, tiled=True),
    )
    vec_float = vec_used.astype(jnp.float32)
    bias_query = vec_float[0:width]
    bias_value = vec_float[width : 2 * width]
    output_bias = vec_float[2 * width : 3 * width]
    up_bias = vec_float[3 * width : 3 * width + FF]
    down_bias = vec_float[3 * width + FF : 4 * width + FF]
    gain_one = vec_float[4 * width + FF : 5 * width + FF]
    shift_one = vec_float[5 * width + FF : 6 * width + FF]
    gain_two = vec_float[6 * width + FF : 7 * width + FF]
    shift_two = vec_float[7 * width + FF : 8 * width + FF]
    query_key_value_weight = attn_used[:, : 3 * width]
    output_weight = attn_used[:, 3 * width :]
    up_weight = ffn_used[:, :FF]
    down_weight = ffn_used[:, FF:]
    column_scale = jnp.concatenate(
        [jnp.full((width,), head_dim ** (-0.5), jnp.float32), jnp.ones((2 * width,), jnp.float32)]
    )
    flat_in = tokens.reshape(tok_rows, width)
    query_key_value_bias = jnp.concatenate(
        [bias_query, jnp.zeros((width,), jnp.float32), bias_value]
    )
    query_key_value = (
        (
            jnp.dot(flat_in, query_key_value_weight, preferred_element_type=jnp.float32)
            + query_key_value_bias
        )
        * column_scale
    ).astype(jnp.bfloat16)
    head_split = lax.all_to_all(
        query_key_value.reshape(seq_count, half_len, 3, seq_parts, head_width),
        "seq",
        split_axis=3,
        concat_axis=1,
        tiled=True,
    )
    shaped = head_split.reshape(seq_count, full_len, 3, heads_here, head_dim)
    query_all = shaped[:, :, 0]
    key_all = shaped[:, :, 1]
    value_all = shaped[:, :, 2]
    live_mask = jnp.arange(full_len)[None, :] < slot_len[:, None]
    context_rows, log_total = lax.map(attend_forward, (query_all, key_all, value_all, live_mask))
    token_split = lax.all_to_all(
        context_rows.reshape(seq_count, full_len, 1, head_width),
        "seq",
        split_axis=1,
        concat_axis=2,
        tiled=True,
    )
    ctx_rows = token_split.reshape(tok_rows, width)
    attended_rows = (
        jnp.dot(ctx_rows, output_weight, preferred_element_type=jnp.float32) + output_bias
    )
    hidden_state, normed_one, inverse_one = norm_forward(
        flat_in.astype(jnp.float32) + attended_rows, gain_one, shift_one
    )
    hidden_low = hidden_state.astype(jnp.bfloat16)
    pre_activation = jnp.dot(hidden_low, up_weight, preferred_element_type=jnp.float32) + up_bias
    active_units = gelu_exact(pre_activation).astype(jnp.bfloat16)
    branch_output = contract_cols(active_units, down_weight) + down_bias
    result, normed_two, inverse_two = norm_forward(
        hidden_state + branch_output, gain_two, shift_two
    )
    layer_out = result.astype(jnp.bfloat16).reshape(seq_count, half_len, width)
    upstream = cotangent.reshape(tok_rows, width).astype(jnp.float32)
    grad_gain_two = jnp.sum(upstream * normed_two, axis=0)
    grad_shift_two = jnp.sum(upstream, axis=0)
    grad_resid_two = norm_backward(upstream, normed_two, inverse_two, gain_two)
    grad_branch = grad_resid_two.astype(jnp.bfloat16)
    grad_bias_down = jnp.sum(grad_branch.astype(jnp.float32), axis=0)
    grad_w_down = contract_rows(grad_branch, active_units)
    grad_active = jnp.dot(grad_branch, down_weight, preferred_element_type=jnp.float32)
    unused, gelu_pull = jax.vjp(gelu_exact, pre_activation)
    grad_pre = gelu_pull(grad_active)[0].astype(jnp.bfloat16)
    grad_bias_up = jnp.sum(grad_pre.astype(jnp.float32), axis=0)
    grad_w_up = contract_rows(hidden_low, grad_pre)
    grad_hidden = grad_resid_two + contract_cols(grad_pre, up_weight)
    grad_gain_one = jnp.sum(grad_hidden * normed_one, axis=0)
    grad_shift_one = jnp.sum(grad_hidden, axis=0)
    grad_resid_one = norm_backward(grad_hidden, normed_one, inverse_one, gain_one)
    grad_attended = grad_resid_one.astype(jnp.bfloat16)
    grad_bias_out = jnp.sum(grad_attended.astype(jnp.float32), axis=0)
    grad_w_out = contract_rows(ctx_rows, grad_attended)
    grad_ctx = contract_cols(grad_attended, output_weight).astype(jnp.bfloat16)
    ctx_heads = lax.all_to_all(
        grad_ctx.reshape(seq_count, half_len, seq_parts, head_width),
        "seq",
        split_axis=2,
        concat_axis=1,
        tiled=True,
    )
    grad_heads = lax.map(
        attend_backward,
        (
            query_all,
            key_all,
            value_all,
            live_mask,
            log_total,
            ctx_heads.reshape(seq_count, full_len, heads_here, head_dim),
        ),
    )
    grad_tokens = lax.all_to_all(
        grad_heads.reshape(seq_count, full_len, 3, 1, head_width),
        "seq",
        split_axis=1,
        concat_axis=3,
        tiled=True,
    )
    grad_qkv = (grad_tokens.reshape(tok_rows, 3 * width).astype(jnp.float32) * column_scale).astype(
        jnp.bfloat16
    )
    grad_qkv_float = grad_qkv.astype(jnp.float32)
    grad_bias_query = jnp.sum(grad_qkv_float[:, :width], axis=0)
    grad_bias_value = jnp.sum(grad_qkv_float[:, 2 * width :], axis=0)
    grad_w_qkv = contract_rows(flat_in, grad_qkv)
    input_grad = (grad_resid_one + contract_cols(grad_qkv, query_key_value_weight)).reshape(
        seq_count, half_len, width
    )
    grad_vector = jnp.concatenate(
        [
            grad_bias_query,
            grad_bias_value,
            grad_bias_out,
            grad_bias_up,
            grad_bias_down,
            grad_gain_one,
            grad_shift_one,
            grad_gain_two,
            grad_shift_two,
        ]
    )
    attn_grad_full = jnp.concatenate([grad_w_qkv, grad_w_out], axis=1)
    attn_sum, ffn_sum, vector_sum = (
        lax.psum_scatter(attn_grad_full, ("dp", "seq"), scatter_dimension=1, tiled=True),
        lax.psum_scatter(
            jnp.concatenate([grad_w_up, grad_w_down], axis=1),
            ("dp", "seq"),
            scatter_dimension=1,
            tiled=True,
        ),
        lax.psum_scatter(grad_vector, ("dp", "seq"), scatter_dimension=0, tiled=True),
    )
    shard_index = lax.axis_index(("dp", "seq"))
    attn_cols = shard_index * attn_weights.shape[1] + jnp.arange(attn_weights.shape[1])
    attn_rate = jnp.where(
        attn_cols < 2 * width, math.sqrt(2.0), jnp.where(attn_cols < 3 * width, 1.5, 1.8)
    ) * width ** (-0.5)
    ffn_cols = shard_index * ffn_weights.shape[1] + jnp.arange(ffn_weights.shape[1])
    ffn_rate = jnp.where(ffn_cols < FF, width ** (-0.5), 1.5 * FF ** (-0.5))
    attn_m, attn_v, attn_new = adam_update(
        attn_weights, attn_moment, attn_second, attn_sum, attn_rate[None, :]
    )
    ffn_m, ffn_v, ffn_new = adam_update(
        ffn_weights, ffn_moment, ffn_second, ffn_sum, ffn_rate[None, :]
    )
    vec_m, vec_v, vec_new = adam_update(
        vectors, vector_moment, vector_second, vector_sum, vector_rate
    )
    return (
        layer_out,
        input_grad,
        attn_m,
        attn_v,
        attn_new,
        attn_new.astype(jnp.bfloat16),
        ffn_m,
        ffn_v,
        ffn_new,
        ffn_new.astype(jnp.bfloat16),
        vec_m,
        vec_v,
        vec_new,
        vec_new.astype(jnp.bfloat16),
    )


def solution(mesh):
    placed = (
        P("dp", "seq", None),
        P("dp", "seq", None),
        P("dp", None),
        P("dp", None),
        P(None, ("dp", "seq")),
        P(None, ("dp", "seq")),
        P(None, ("dp", "seq")),
        P(None, ("dp", "seq")),
        P(None, ("dp", "seq")),
        P(None, ("dp", "seq")),
        P(("dp", "seq")),
        P(("dp", "seq")),
        P(("dp", "seq")),
    )
    return jax.shard_map(
        local,
        mesh=mesh,
        in_specs=placed,
        out_specs=(
            P("dp", "seq", None),
            P("dp", "seq", None),
            P(None, ("dp", "seq")),
            P(None, ("dp", "seq")),
            P(None, ("dp", "seq")),
            P(None, ("dp", "seq")),
            P(None, ("dp", "seq")),
            P(None, ("dp", "seq")),
            P(None, ("dp", "seq")),
            P(None, ("dp", "seq")),
            P(("dp", "seq")),
            P(("dp", "seq")),
            P(("dp", "seq")),
            P(("dp", "seq")),
        ),
        check_vma=False,
    )
```

profile of v0, /device:TPU:0, one launch (start us, length us, event | category | flops | bytes accessed | tf_op | source)
XLA Modules:
  0.0 747.6 jit_solution(9958369213726310925)
XLA Ops:
  11.7 42.3 %all-reduce = bf16[9216]{0:T(1024)(128)(2,1)S(1)} all-reduce(bf16[9216]{0:T(1024)(128)(2,1)S(1)} %dynamic-update-slice), channel_id=1, replica_groups=mesh['dp'=16,'seq'=2] {'dp','seq'}, use_global_device_ids=true, to_apply=%add | all-reduce | flops 9216 | bytes 36864
  59.1 19.2 %all-gather.3.cloned.1.call-done = bf16[768,3072]{0,1:T(8,128)(2,1)} async-done(((bf16[768,96]{0,1:T(8,128)(2,1)}), bf16[768,3072]{0,1:T(8,128)(2,1)}) %all-gather.3.cloned.1.call-update) | async-done | bytes 4718608 | tf_op jit(solution)/shard_map/all_gather | solution.py:124
  78.3 8.5 %multiply_convert_fusion.4 = bf16[1024,2304]{1,0:T(8,128)(2,1)} fusion(bf16[1024,768]{1,0:T(8,128)(2,1)} %bitcast.185, f32[2304]{0:T(1024)} %constant.40.clone.1, f32[2304]{0:T(1024)S(1)} %pad_maximum_fusion.2, bf16[768,3072]{0,1:T(8,128)(2,1)} %all-gather.3.cloned.1.call-done), kind=kOutput, calls=%fused_computation.79 | convolution fusion | flops 3630956544 | bytes 9851904 | tf_op jit(solution)/shard_map/dot_general | solution.py:151
  86.8 9.9 %reshape.235 = bf16[4,256,3,2,384]{4,3,2,1,0:T(2,128)(2,1)} reshape(bf16[1024,2304]{1,0:T(8,128)(2,1)} %multiply_convert_fusion.4) | data formatting | bytes 9437184 | tf_op jit(solution)/shard_map/reshape | solution.py:157
  96.7 3.3 copy.177
  100.0 8.6 %all_to_all.54 = bf16[4,256,3,2,384]{4,1,2,0,3:T(8,128)(2,1)} all-to-all(bf16[4,256,3,2,384]{4,1,2,0,3:T(8,128)(2,1)S(1)} %copy.177), channel_id=1, replica_groups=mesh['dp'=16,'seq'=2] {'seq'}, dimensions={3} | all-to-all | bytes 9437184 | tf_op jit(solution)/shard_map/all_to_all | solution.py:156
  108.5 12.4 %copy.178 = bf16[4,2,256,3,1,384]{2,1,5,3,0,4:T(2,128)(2,1)} copy(bf16[4,2,256,3,1,384]{5,2,3,0,1,4:T(8,128)(2,1)} %bitcast.176) | data formatting | bytes 9437184 | tf_op jit(solution)/shard_map/all_to_all | solution.py:156
  121.0 8.6 %reshape.236 = bf16[4,512,3,6,64]{1,4,3,2,0:T(8,128)(2,1)} reshape(bf16[4,2,256,3,1,384]{2,1,5,3,0,4:T(2,128)(2,1)} %copy.178) | data formatting | bytes 9437184 | tf_op jit(solution)/shard_map/reshape | solution.py:163
  129.5 4.6 slice_bitcast_fusion
  134.1 25.7 %while.22 = (s32[]{:T(128)}, bf16[4,512,6,64]{1,3,2,0:T(8,128)(2,1)}, f32[4,6,512,1]{2,1,3,0:T(8,128)}, bf16[4,512,6,64]{1,3,2,0:T(8,128)(2,1)}, pred[4,512]{1,0...) while((s32[]{:T(128)}, ...), condition=%wide.region_4.5_spmd, body=%wide.region_1.4_spmd.sunk | while | flops 417002496 | bytes 20554840 | solution.py:168
  137.3 3.3 fusion.131
  143.7 3.3 fusion.131
  150.1 3.3 fusion.131
  156.5 3.3 fusion.131
  159.8 4.1 copy.179
  163.9 6.3 all_to_all.55
  172.4 3.4 fusion.103
  176.4 36.9 %multiply_convert_fusion.1 = (bf16[1024,3072]{1,0:T(8,128)(2,1)S(1)}, f32[1024,3072]{1,0:T(8,128)}, f32[1024,3072]{1,0:T(8,128)}) fusion(f32[3072]{0:T(1024)S(1)} %slice.83, bf16[768,6144]{0,1:T(8,128)(2,1)} %all-gather.5.cloned.1.call-done, f32[1024,768]{1,0:T(8,128)S(1)} %get-tuple-element.284, f32[768]{0:T(1024)S(1)} %get-tuple-element.279, ...), kind=kOutput, calls=%fused_computation.61 | convolution fusion | flops 5043388416 | bytes 39348224 | tf_op jit(solution)/shard_map/dot_general | solution.py:184
  213.4 5.4 fusion.104
  221.2 3.5 convert_reduce_fusion.2
  224.7 19.4 %convert_reduce_fusion = (f32[3072]{0:T(1024)}, bf16[1024,3072]{1,0:T(8,128)(2,1)}) fusion(f32[1024,3072]{1,0:T(8,128)} %get-tuple-element.266, bf16[768,6144]{0,1:T(8,128)(2,1)} %all-gather.5.cloned.1.call-done, f32[1024,768]{1,0:T(8,128)} %get-tuple-element.254, f32[1024,3072]{1,0:T(8,128)} %get-tuple-element.285, f32[3072]{0:T(1024)S(1)} %slice.83), kind=kOutput, calls=%fused_computation.59 | convolution fusion | flops 4886098944 | bytes 39346176 | tf_op jit(solution)/shard_map/dot_general | solution.py:198
  244.1 10.5 %multiply_reduce_fusion.1 = (f32[768]{0:T(1024)}, f32[1024]{0:T(1024)S(1)}, f32[1024]{0:T(1024)S(1)}, f32[768]{0:T(1024)}, f32[1024,768]{1,0:T(8,128)S(1)}) fusion(f32[1024,768]{1,0:T(8,128)S(1)} %get-tuple-element.284, f32[1024]{0:T(1024)S(1)} %add_rsqrt_fusion.1, f32[1024]{0:T(1024)S(1)} %broadcast_multiply_fusion.4, f32[768]{0:T(1024)S(1)} %get-tuple-element.278, ...), kind=kOutput, calls=%fused_computation.101 | convolution fusion | flops 4839698432 | bytes 20472832 | tf_op jit(solution)/shard_map/dot_general | solution.py:41
  262.6 6.3 all_to_all.56
  268.9 4.9 copy.183
  273.8 3.8 reshape.241
  277.6 44.7 %while.23 = (s32[]{:T(128)}, bf16[4,512,3,384]{1,3,2,0:T(8,128)(2,1)}, bf16[4,512,6,64]{1,3,2,0:T(8,128)(2,1)S(1)}, pred[4,512]{1,0:T(4,128)(4,1)S(1)}, bf16[4,5...) while((s32[]{:T(128)}, ...), condition=%wide.region_15.16_spmd, body=%wide.region_13.15_spmd.sunk | while | flops 1029633024 | bytes 59868300 | solution.py:218
  290.6 2.9 multiply_reduce_fusion.7
  301.7 2.9 multiply_reduce_fusion.7
  312.9 2.9 multiply_reduce_fusion.7
  322.3 8.5 %copy.184 = bf16[4,512,3,384]{3,0,2,1:T(4,128)(2,1)} copy(bf16[4,512,3,384]{1,3,2,0:T(8,128)(2,1)} %get-tuple-element.96) | data formatting | bytes 9437184 | tf_op jit(solution)/shard_map/while | solution.py:218
  330.8 9.2 %all_to_all.57 = bf16[4,512,3,1,384]{4,0,3,2,1:T(4,128)(2,1)S(1)} all-to-all(bf16[4,512,3,1,384]{4,0,3,2,1:T(4,128)(2,1)} %bitcast.177), channel_id=1, replica_groups=mesh['dp'=16,'seq'=2] {'seq'}, dimensions={1} | all-to-all | bytes 9437184 | tf_op jit(solution)/shard_map/all_to_all | solution.py:229
  339.9 5.0 convert.21
  345.0 16.9 %multiply_convert_fusion.2 = bf16[4,256,3,2,1,384]{5,3,2,1,0,4:T(2,128)(2,1)} fusion(f32[3,2,384]{2,1,0:T(2,128)S(1)} %copy-done.29, f32[4,2,256,3,1,384]{5,0,3,2,1,4:T(4,128)} %convert.21), kind=kLoop, calls=%fused_computation.77 | loop fusion | flops 4718592 | bytes 14164992 | tf_op jit(solution)/shard_map/convert_element_type | solution.py:236
  361.9 11.3 %convert_element_type.142 = bf16[1024,2304]{1,0:T(8,128)(2,1)} reshape(bf16[4,256,3,2,1,384]{5,3,2,1,0,4:T(2,128)(2,1)} %multiply_convert_fusion.2) | data formatting | bytes 9437184 | tf_op jit(solution)/shard_map/convert_element_type | solution.py:236
  373.2 8.3 %convolution_bitcast_fusion = f32[768,2304]{0,1:T(8,128)} fusion(bf16[1024,2304]{1,0:T(8,128)(2,1)} %convert_element_type.142, bf16[1024,768]{1,0:T(8,128)(2,1)S(1)} %bitcast.187), kind=kOutput, calls=%fused_computation.80 | convolution fusion | flops 3623878656 | bytes 13369344 | tf_op jit(solution)/shard_map/dot_general | solution.py:35
  381.5 7.2 pad_maximum_fusion.1
  388.8 8.7 %fusion.88 = f32[768,3072]{1,0:T(8,128)S(1)} fusion(bf16[1024,3072]{1,0:T(8,128)(2,1)} %copy-done.39, f32[1024,768]{1,0:T(8,128)} %get-tuple-element.254), kind=kOutput, calls=%fused_computation.168 | convolution fusion | flops 4832624640 | bytes 18874368 | tf_op jit(solution)/shard_map/dot_general | solution.py:35
  397.5 8.1 %fusion.91 = f32[768,3072]{1,0:T(8,128)S(1)} fusion(bf16[1024,3072]{1,0:T(8,128)(2,1)} %get-tuple-element.290, f32[1024,768]{1,0:T(8,128)S(1)} %copy-done.6, f32[768]{0:T(1024)S(1)} %copy-done.20, f32[768]{0:T(1024)S(1)} %get-tuple-element.278, f32[1024]{0:T(1024)S(1)} %add_rsqrt_fusion.1, f32[1024]{0:T(1024)S(1)} %broadcast_multiply_fusion.4), kind=kOutput, calls=%fused_computation.171 | convolution fusion | flops 4835770368 | bytes 18888704 | tf_op jit(solution)/shard_map/dot_general | solution.py:35
  405.6 7.1 pad_maximum_fusion
  412.7 19.2 %copy.192 = f32[768,6144]{0,1:T(8,128)} copy(f32[768,6144]{1,0:T(8,128)} %pad_maximum_fusion) | data formatting | bytes 37748736
  431.9 10.8 %copy.199 = f32[4,2,256,3,1,384]{5,1,3,2,0,4:T(2,128)} copy(bf16[4,2,256,3,1,384]{5,0,3,2,1,4:T(4,128)(2,1)} %bitcast.171) | data formatting | bytes 14155776 | tf_op jit(solution)/shard_map/convert_element_type | solution.py:236
  442.7 12.7 %reshape.245 = f32[1024,2304]{1,0:T(8,128)} reshape(f32[4,256,3,2,1,384]{5,3,2,1,0,4:T(2,128)} %bitcast.175) | data formatting | bytes 18874368 | tf_op jit(solution)/shard_map/convert_element_type | solution.py:236
  455.5 4.4 fusion.70
  460.8 40.6 %all-reduce.1 = f32[9216]{0:T(1024)S(1)} all-reduce(f32[9216]{0:T(1024)S(1)} %constant_dynamic-update-slice_fusion), channel_id=4, replica_groups=mesh['dp'=16,'seq'=2] {'dp','seq'}, use_global_device_ids=true, to_apply=%region_27.28.clone | all-reduce | flops 9216 | bytes 73728
  502.1 10.3 %fusion.71 = f32[1024,768]{1,0:T(8,128)} fusion(f32[1024,768]{1,0:T(8,128)S(1)} %copy-done.10, bf16[768,3072]{0,1:T(8,128)(2,1)} %all-gather.3.cloned.1.call-done, f32[1024,2304]{1,0:T(8,128)} %reshape.245, f32[2304]{0:T(1024)S(1)} %copy-done.27), kind=kOutput, calls=%fused_computation.120 | convolution fusion | flops 3629383680 | bytes 19276800 | tf_op jit(solution)/shard_map/dot_general | solution.py:41
  512.4 11.7 %reduce-scatter.5.cloned.1.call-done = f32[768,96]{0,1:T(8,128)} async-done(((f32[768,3072]{0,1:T(8,128)}), f32[768,96]{0,1:T(8,128)}) %reduce-scatter.5.cloned.1.call-update) | async-done | bytes 294928 | tf_op jit(solution)/shard_map/reduce_scatter | solution.py:261
  526.3 211.0 %reduce-scatter.7.cloned.1.call-done = f32[192,768]{1,0:T(8,128)} async-done(((f32[6144,768]{1,0:T(8,128)}), f32[192,768]{1,0:T(8,128)}) %reduce-scatter.7.cloned.1.call-update) | async-done | bytes 589840
  737.3 3.2 fusion.97
  (193 shorter events, 74.3 us)
Async XLA Ops:
  7.2 71.1 %all-gather.3.cloned.1.call-start = ((), (), s32[]{:S(2)}) async-start(), calls=%async_computation.6 | async-start | bytes 4866048 | tf_op jit(solution)/shard_map/all_gather | solution.py:124
  8.9 167.5 %all-gather.5.cloned.1.call-start = ((), (), s32[]{:S(2)}) async-start(), calls=%async_computation.7 | async-start | bytes 9732096 | tf_op jit(solution)/shard_map/all_gather | solution.py:125
  10.8 513.3 %reduce-scatter.5.cloned.1.call-start = ((), (), s32[]{:S(2)}) async-start(), calls=%async_computation.8 | async-start | bytes 9732096 | tf_op jit(solution)/shard_map/reduce_scatter | solution.py:261
  54.7 32.1 %copy-start.17 = (f32[768]{0:T(1024)}, f32[768]{0:T(1024)S(1)}, u32[]{:S(2)}) copy-start(f32[768]{0:T(1024)S(1)} %get-tuple-element.275) | copy-start | bytes 9220
  54.7 158.7 %copy-start.19 = (f32[768]{0:T(1024)}, f32[768]{0:T(1024)S(1)}, u32[]{:S(2)}) copy-start(f32[768]{0:T(1024)S(1)} %get-tuple-element.279) | copy-start | bytes 9220
  159.8 10.6 %copy-start.1 = (bf16[4,512,6,64]{1,3,2,0:T(8,128)(2,1)}, bf16[4,512,6,64]{1,3,2,0:T(8,128)(2,1)S(1)}, u32[]{:S(2)}) copy-start(bf16[4,512,6,64]{1,3,2,0:T(8,128)(2,1)S(1)} %get-tuple-element.452) | copy-start | bytes 4718596
  159.8 10.6 %copy-start.3 = (bf16[4,512,6,64]{1,3,2,0:T(8,128)(2,1)}, bf16[4,512,6,64]{1,3,2,0:T(8,128)(2,1)S(1)}, u32[]{:S(2)}) copy-start(bf16[4,512,6,64]{1,3,2,0:T(8,128)(2,1)S(1)} %get-tuple-element.453) | copy-start | bytes 4718596
  159.8 10.6 %copy-start.15 = (pred[4,512]{1,0:T(4,128)(4,1)}, pred[4,512]{1,0:T(4,128)(4,1)S(1)}, u32[]{:S(2)}) copy-start(pred[4,512]{1,0:T(4,128)(4,1)S(1)} %get-tuple-element.461) | copy-start | bytes 6148
  170.2 2.2 copy-start.37
  172.4 3.5 copy-start.12
  175.9 78.8 %copy-start.5 = (f32[1024,768]{1,0:T(8,128)}, f32[1024,768]{1,0:T(8,128)S(1)}, u32[]{:S(2)}) copy-start(f32[1024,768]{1,0:T(8,128)S(1)} %get-tuple-element.284) | copy-start | bytes 9437188
  176.4 36.9 %copy-start.31 = (f32[768]{0:T(1024)S(1)}, f32[768]{0:T(1024)}, u32[]{:S(2)}) copy-start(f32[768]{0:T(1024)} %get-tuple-element.277) | copy-start | bytes 9220
  176.4 36.9 %copy-start.36 = (bf16[768,6144]{0,1:T(8,128)(2,1)S(1)}, bf16[768,6144]{0,1:T(8,128)(2,1)}, u32[]{:S(2)}) copy-start(bf16[768,6144]{0,1:T(8,128)(2,1)} %all-gather.5.cloned.1.call-done) | copy-start | bytes 28311556
  213.3 5.5 copy-start.39
  213.4 6.0 copy-start.8
  213.4 6.0 copy-start.18
  218.8 2.4 copy-start.21
  218.8 2.4 copy-start.23
  254.6 1.7 copy-start.13
  256.4 2.9 copy-start.9
  262.6 15.0 %copy-start.2 = (bf16[4,512,6,64]{1,3,2,0:T(8,128)(2,1)S(1)}, bf16[4,512,6,64]{1,3,2,0:T(8,128)(2,1)}, u32[]{:S(2)}) copy-start(bf16[4,512,6,64]{1,3,2,0:T(8,128)(2,1)} %copy-done.1) | copy-start | bytes 4718596
  262.6 15.0 %copy-start.4 = (bf16[4,512,6,64]{1,3,2,0:T(8,128)(2,1)S(1)}, bf16[4,512,6,64]{1,3,2,0:T(8,128)(2,1)}, u32[]{:S(2)}) copy-start(bf16[4,512,6,64]{1,3,2,0:T(8,128)(2,1)} %copy-done.3) | copy-start | bytes 4718596
  262.6 15.0 %copy-start.16 = (pred[4,512]{1,0:T(4,128)(4,1)S(1)}, pred[4,512]{1,0:T(4,128)(4,1)}, u32[]{:S(2)}) copy-start(pred[4,512]{1,0:T(4,128)(4,1)} %copy-done.15) | copy-start | bytes 6148
  277.6 1.8 copy-start.7
  288.8 1.8 copy-start.7
  299.9 1.8 copy-start.7
  311.1 1.8 copy-start.7
  339.9 5.0 copy-start
  339.9 5.0 copy-start.29
  361.9 11.3 %copy-start.38 = (bf16[4,256,768]{2,1,0:T(8,128)(2,1)S(1)}, bf16[4,256,768]{2,1,0:T(8,128)(2,1)}, u32[]{:S(2)}) copy-start(bf16[4,256,768]{2,1,0:T(8,128)(2,1)} %param.17) | copy-start | bytes 4718596
  373.2 8.3 %copy-start.11 = (f32[768,768]{0,1:T(8,128)S(1)}, f32[768,768]{0,1:T(8,128)}, u32[]{:S(2)}) copy-start(f32[768,768]{0,1:T(8,128)} %fusion.85) | copy-start | bytes 7077892
  388.7 8.8 %copy-start.6 = (f32[1024,768]{1,0:T(8,128)S(1)}, f32[1024,768]{1,0:T(8,128)}, u32[]{:S(2)}) copy-start(f32[1024,768]{1,0:T(8,128)} %copy-done.5) | copy-start | bytes 9437188
  388.7 8.8 %copy-start.20 = (f32[768]{0:T(1024)S(1)}, f32[768]{0:T(1024)}, u32[]{:S(2)}) copy-start(f32[768]{0:T(1024)} %copy-done.19) | copy-start | bytes 9220
  388.7 348.6 %reduce-scatter.7.cloned.1.call-start = ((), (), s32[]{:S(2)}) async-start(), calls=%async_computation.9 | async-start | bytes 19464192
  442.7 12.7 %copy-start.27 = (f32[2304]{0:T(1024)S(1)}, f32[2304]{0:T(1024)}, u32[]{:S(2)}) copy-start(f32[2304]{0:T(1024)} %constant.40.clone.1) | copy-start | bytes 27652
  459.9 0.7 copy-start.25
  459.9 0.7 copy-start.28
  459.9 0.7 copy-start.22
  460.0 0.7 copy-start.33
  460.0 0.7 copy-start.32
  460.0 0.7 copy-start.26
  460.0 0.7 copy-start.24
  460.0 41.3 %copy-start.30 = (f32[288]{0:T(512)S(1)}, f32[288]{0:T(512)}, u32[]{:S(2)}) copy-start(f32[288]{0:T(512)} %param.27) | copy-start | bytes 3460
  460.0 41.3 %copy-start.34 = (f32[288]{0:T(512)S(1)}, f32[288]{0:T(512)}, u32[]{:S(2)}) copy-start(f32[288]{0:T(512)} %param.29) | copy-start | bytes 3460
  460.0 41.3 %copy-start.35 = (f32[288]{0:T(512)S(1)}, f32[288]{0:T(512)}, u32[]{:S(2)}) copy-start(f32[288]{0:T(512)} %param.28) | copy-start | bytes 3460
  460.0 42.0 %copy-start.10 = (f32[1024,768]{1,0:T(8,128)S(1)}, f32[1024,768]{1,0:T(8,128)}, u32[]{:S(2)}) copy-start(f32[1024,768]{1,0:T(8,128)} %copy-done.9) | copy-start | bytes 9437188
  502.1 22.0 %copy-start.14 = (f32[768,96]{0,1:T(8,128)S(1)}, f32[768,96]{0,1:T(8,128)}, u32[]{:S(2)}) copy-start(f32[768,96]{0,1:T(8,128)} %param.21) | copy-start | bytes 884740
Sparse Core Ops, SparseCore 0:
  11.5 66.7 all-gather.2
  81.8 80.5 all-gather.4
  388.8 135.2 reduce-scatter.4
  531.5 205.7 reduce-scatter.6
where the time goes:
time: 759 us; the launch traced here: 748 us
  waiting for transfers between devices  242 us (32%)
  matrix products  172 us (23%)
  local copies, waits for them, and re-layouts  122 us (16%)
  blocking collectives  113 us (15%)
  other arithmetic  83.3 us (11%)
  between operations  15 us (2%)
    unnamed x5, waiting for transfers between devices  211 us
    unnamed x2, blocking collectives  82.9 us
    dot_general x1, matrix products, local(): jnp.dot(hidden_low, up_weight, preferred_element_type=jnp.float32) + up_bias  36.9 us
    dot_general x4, matrix products, contract_cols(): lax.dot_general(left, right, (((1,), (1,)), ((), ())), preferred_element_...  29 us
    dot_general x4, matrix products, contract_rows(): lax.dot_general(left, right, (((0,), (0,)), ((), ())), preferred_element_...  28 us
    convert_element_type x2, local copies, waits for them, and re-layouts, local(): grad_tokens.reshape(tok_rows, 3 * width).astype(jnp.float32) * column_scale  23.5 us
    unnamed x91, local copies, waits for them, and re-layouts  20.7 us
    dot_general x1, matrix products, local(): jnp.dot(grad_branch, down_weight, preferred_element_type=jnp.float32)  19.4 us
  transfers between devices with their start and end apart: 4, of which 3 were waited for; matrix products, arithmetic and copies ran while one was open for 23% of the time, Pallas kernels for 0%

commit v1 on v0

v1 whole, which is shorter than its diff:
```python
import math

import jax
import jax.numpy as jnp
from jax import lax
from jax.experimental import pallas as pl
from jax.experimental.pallas import tpu as pltpu
from jax.sharding import PartitionSpec as P

H = 12
FF = 3072
STEP = 5

epsilon = 1e-06
masked_score = -1e30
decay_rate = 0.5
adam_epsilon = 1e-08
weight_decay = 0.01
vector_rate = 0.5

AXES = ("dp", "seq")
BF = jnp.bfloat16
F32 = jnp.float32
VMEM_LIMIT = 56 * 1024 * 1024
TILE = 256
COST = 16
ANY = pl.BlockSpec(memory_space=pl.ANY)
SMEM = pl.BlockSpec(memory_space=pltpu.SMEM)
VMEM = pl.BlockSpec(memory_space=pltpu.VMEM)


def nn(a, b):
    return lax.dot_general(a, b, (((1,), (0,)), ((), ())), preferred_element_type=F32)


def nt(a, b):
    return lax.dot_general(a, b, (((1,), (1,)), ((), ())), preferred_element_type=F32)


def tn(a, b):
    return lax.dot_general(a, b, (((0,), (0,)), ((), ())), preferred_element_type=F32)


class Grid:
    def __init__(self, chips):
        power = chips.bit_length() - 1
        if 1 << power == chips:
            self.side = 1 << (power // 3)
            self.nz = chips // (self.side * self.side)
        else:
            self.side, self.nz = 1, chips
        self.devices = 2 * chips
        self.xor = 1 << power == chips

    def z_mask(self, m):
        return m * 2 * self.side * self.side

    def x_mask(self, m):
        return 2 * m

    def y_mask(self, m):
        return 2 * m * self.side

    def label(self, core, other, i3, i2, iz):
        x = jnp.where(core == 0, i2, i3)
        y = jnp.where(core == 0, i3, i2)
        return self.z_mask(iz) + self.y_mask(y) + self.x_mask(x) + other


def permute(value, grid, mask_of_core):
    pairs = [(i, i ^ mask_of_core(i & 1)) for i in range(grid.devices)]
    return lax.ppermute(value, AXES, pairs)


def along_two(grid, value, m):
    return permute(value, grid, lambda c: grid.x_mask(m) if c == 0 else grid.y_mask(m))


def along_three(grid, value, m):
    return permute(value, grid, lambda c: grid.y_mask(m) if c == 0 else grid.x_mask(m))


def gather_z(grid, block):
    return [block] + [permute(block, grid, lambda c: grid.z_mask(m)) for m in range(1, grid.nz)]


def gather_two(grid, zed):
    return [zed] + [along_two(grid, zed, m) for m in range(1, grid.side)]


def gather_three(grid, two):
    return [along_three(grid, t, m) for m in range(1, grid.side) for t in two]


def with_core(grid, own):
    return own + [permute(p, grid, lambda c: 1) for p in own]


def is_path(grid, rows):
    return grid.xor and grid.side > 1 and rows % 16 == 0


def slot_of(grid, label, core):
    other = label & 1
    x = (label // 2) & (grid.side - 1)
    y = (label // (2 * grid.side)) & (grid.side - 1)
    z = label // (2 * grid.side * grid.side)
    first = (core ^ other) == 0
    i2 = jnp.where(first, x, y)
    i3 = jnp.where(first, y, x)
    return other, (i3 * grid.side + i2) * grid.nz + z


def natural_vectors(grid, pieces, core, me, row, count):
    side, nz = grid.side, grid.nz
    table = jnp.stack([p[:, row, :count] for p in pieces]).reshape(2, side, side, nz, count)
    turned = jnp.swapaxes(table, 1, 2)
    first = jnp.stack([table[0], turned[1]])
    second = jnp.stack([turned[0], table[1]])
    value = jnp.where(core == 0, first, second)
    value = jnp.transpose(value, (3, 1, 2, 0, 4)).reshape(grid.devices, count)
    bit = 1
    while bit < grid.devices:
        pairs = value.reshape(-1, 2, bit, count)
        value = jnp.where((me & bit) == 0, pairs, pairs[:, ::-1]).reshape(grid.devices, count)
        bit *= 2
    return value.reshape(1, -1).astype(F32)


def start_natural(grid, me_ref, pieces, dest, sems, first=0, last=None):
    last = grid.devices if last is None else last
    rows = dest.shape[0] // (last - first)
    if len(pieces) == 1:
        pltpu.make_async_copy(
            pieces[0].at[pl.ds(first * rows, (last - first) * rows)], dest, sems.at[0]
        ).start()
        return
    me = me_ref[0]
    at = 0
    for other in (0, 1):
        for i3 in range(grid.side):
            for i2 in range(grid.side):
                ref = pieces[at]
                at += 1
                for iz in range(grid.nz):
                    block = me ^ grid.label((me & 1) ^ other, other, i3, i2, iz)

                    def start(block=block, ref=ref, iz=iz):
                        row = pl.multiple_of((block - first) * rows, rows)
                        pltpu.make_async_copy(
                            ref.at[iz, pl.ds(0, rows)], dest.at[pl.ds(row, rows)], sems.at[block]
                        ).start()

                    if last - first == grid.devices:
                        start()
                    else:
                        pl.when((block >= first) & (block < last))(start)


def wait_natural(grid, pieces, dest, sems, begin, end, first=0, last=None):
    last = grid.devices if last is None else last
    rows = dest.shape[0] // (last - first)
    if len(pieces) == 1:
        if begin == first:
            pltpu.make_async_copy(
                pieces[0].at[pl.ds(first * rows, (last - first) * rows)], dest, sems.at[0]
            ).wait()
        return
    for block in range(begin, end):
        pltpu.make_async_copy(
            pieces[0].at[0, pl.ds(0, rows)],
            dest.at[pl.ds((block - first) * rows, rows)],
            sems.at[block],
        ).wait()


def path_shapes(grid, blocks, per, width):
    if not is_path(grid, per):
        return [
            jax.ShapeDtypeStruct((blocks * per, width), BF),
            jax.ShapeDtypeStruct((blocks, 8, width), BF),
        ]
    return [jax.ShapeDtypeStruct((blocks // 2, per, width), BF)] * 2


class Sums:
    def __init__(self, grid, path, keep, send):
        self.grid, self.path, self.keep, self.send = grid, path, keep, send
        self.three, self.two, self.z = [], [], []
        if path:
            self.core = permute(send, grid, lambda c: 1)

    def terms(self, i3, i2, iz):
        grid = self.grid
        base = (i3 * grid.side + i2) * grid.nz
        rows = slice(base + iz.start, base + iz.stop)
        total = self.keep[rows].astype(F32) + self.core[rows].astype(F32)
        if i3 == 0:
            for at, got in self.three:
                if at == i2:
                    total = total + got[iz].astype(F32)
            if i2 == 0:
                for got in self.two:
                    total = total + got[iz].astype(F32)
        return total

    def add_core(self):
        if not self.path:
            return []
        grid = self.grid
        every = slice(0, grid.nz)
        sends = [
            (i2, m, self.terms(m, i2, every).astype(BF))
            for i2 in reversed(range(grid.side))
            for m in range(1, grid.side)
        ]
        self.three = [(i2, along_three(grid, value, m)) for i2, m, value in sends]
        return [value for _, _, value in sends]

    def add_three(self):
        if not self.path:
            return []
        grid = self.grid
        every = slice(0, grid.nz)
        sends = [self.terms(0, m, every).astype(BF) for m in range(1, grid.side)]
        self.two = [along_two(grid, sends[m - 1], m) for m in range(1, grid.side)]
        return sends

    def add_two(self):
        if not self.path:
            return []
        grid = self.grid
        sends = [self.terms(0, 0, slice(m, m + 1))[0].astype(BF) for m in range(1, grid.nz)]
        self.z = [
            permute(sends[m - 1], grid, lambda c: grid.z_mask(m)) for m in range(1, grid.nz)
        ]
        return sends

    def add_z(self):
        if not self.path:
            rows = [v.reshape(-1, v.shape[-1]).astype(F32) for v in (self.keep, self.send)]
            return jnp.concatenate(
                [lax.psum_scatter(v, AXES, scatter_dimension=0, tiled=True) for v in rows]
            )
        total = self.terms(0, 0, slice(0, 1))[0]
        for got in self.z:
            total = total + got.astype(F32)
        return total


def params(**more):
    return pltpu.CompilerParams(vmem_limit_bytes=VMEM_LIMIT, **more)


def cost(macs, bytes_accessed, trans=0):
    return pl.CostEstimate(
        flops=2 * macs // COST, bytes_accessed=bytes_accessed // COST, transcendentals=trans // COST
    )


def rows_spec(width, tile=TILE):
    return pl.BlockSpec((tile, width), lambda i: (i, 0))


def whole(shape):
    zeros = (0,) * len(shape)
    return pl.BlockSpec(shape, lambda *i: zeros)


def fixed(*shape):
    zeros = (0,) * len(shape)
    return pl.BlockSpec(shape, lambda i: zeros)


def norm_rows(values):
    center = values - jnp.mean(values, axis=-1, keepdims=True)
    inverse = lax.rsqrt(jnp.mean(center * center, axis=-1, keepdims=True) + epsilon)
    return center * inverse, inverse


def norm_back(upstream, normed, inverse, gain):
    u = upstream * gain
    centered = u - jnp.mean(u, axis=-1, keepdims=True)
    return inverse * (centered - normed * jnp.mean(u * normed, axis=-1, keepdims=True))


def gelu_pair(u):
    z = jnp.abs(u) * math.sqrt(0.5)
    e = jnp.exp(-0.5 * u * u)
    t = 1.0 / (1.0 + 0.3275911 * z)
    poly = t * (
        0.254829592
        + t * (-0.284496736 + t * (1.421413741 + t * (-1.453152027 + t * 1.061405429)))
    )
    tail = 0.5 * poly * e
    phi = jnp.where(u >= 0, 1.0 - tail, tail)
    return u * phi, phi + u * (e * (1.0 / math.sqrt(2.0 * math.pi)))


def load_sequences(core, mine, others, dest, sems):
    count = mine.shape[0] // 2
    half = mine.shape[1]
    copies = []
    for s in range(count):
        seq = core * count + s
        for i, src in enumerate((mine, others)):
            at = s * 2 * half + (core ^ i) * half
            copies.append(
                pltpu.make_async_copy(
                    src.at[seq], dest.at[pl.ds(pl.multiple_of(at, half), half)], sems.at[2 * s + i]
                )
            )
    for copy in copies:
        copy.start()
    return copies


def store_sequences(core, src, mine, others, sems):
    count, half = others.shape[0], others.shape[1]
    copies = []
    for s in range(count):
        for i, dest in enumerate((mine.at[core * count + s], others.at[s])):
            at = s * 2 * half + (core ^ i) * half
            copies.append(
                pltpu.make_async_copy(
                    src.at[pl.ds(pl.multiple_of(at, half), half)], dest, sems.at[2 * s + i]
                )
            )
    for copy in copies:
        copy.start()
    return copies


def qkv_kernel(grid, me_ref, vec_ref, mine, others, *rest):
    pieces, (out_hbm, x_hbm, w, x, out, wsem, xsem, osem) = rest[:-8], rest[-8:]
    rows, width = x.shape
    scale = (width // H) ** -0.5
    core = me_ref[0] & 1
    loads = load_sequences(core, mine, others, x, xsem)
    blocks = grid.devices // 4
    start_natural(grid, me_ref, pieces, w, wsem, 0, 3 * blocks)
    for copy in loads:
        copy.wait()
    stores = [pltpu.make_async_copy(x, x_hbm, osem.at[3])]
    stores[0].start()
    for part in range(3):
        wait_natural(
            grid, pieces, w, wsem, part * blocks, (part + 1) * blocks, 0, 3 * blocks
        )
        cols = slice(part * width, (part + 1) * width)

        @pl.loop(0, rows // TILE)
        def _(r):
            at = pl.ds(pl.multiple_of(r * TILE, TILE), TILE)
            z = nt(x[at, :], w[cols, :])
            if part == 0:
                z = (z + vec_ref[:, 0:width]) * scale
            if part == 2:
                z = z + vec_ref[:, width : 2 * width]
            out[at, cols] = z.astype(BF)

        copy = pltpu.make_async_copy(out.at[:, cols], out_hbm.at[:, cols], osem.at[part])
        copy.start()
        stores.append(copy)
    for copy in stores:
        copy.wait()


def qkv_call(grid, me, vec, mine, others, pieces):
    width = mine.shape[2]
    rows = mine.shape[0] * mine.shape[1]
    return pl.pallas_call(
        lambda *r: qkv_kernel(grid, *r),
        in_specs=[SMEM, VMEM, ANY, ANY] + [ANY] * len(pieces),
        out_specs=[ANY, ANY],
        out_shape=[
            jax.ShapeDtypeStruct((rows, 3 * width), BF),
            jax.ShapeDtypeStruct((rows, width), BF),
        ],
        scratch_shapes=[
            pltpu.VMEM((3 * width, width), BF),
            pltpu.VMEM((rows, width), BF),
            pltpu.VMEM((rows, 3 * width), BF),
            pltpu.SemaphoreType.DMA((grid.devices,)),
            pltpu.SemaphoreType.DMA((mine.shape[0],)),
            pltpu.SemaphoreType.DMA((4,)),
        ],
        compiler_params=params(),
        cost_estimate=cost(rows * width * 3 * width, 12 << 20),
        name="qkv",
    )(me, vec, mine, others, *pieces)


def vector_refs(vec_ref, width):
    tail = 3 * width + FF
    found = [vec_ref[:, 2 * width : 3 * width], vec_ref[:, 3 * width : tail]]
    return found + [vec_ref[:, tail + i * width : tail + (i + 1) * width] for i in range(5)]


def attend_kernel(grid, npieces, seq, len_ref, me_ref, q_ref, k_ref, v_ref, x_ref, vec_ref, *rest):
    pieces = rest[:npieces]
    quarter = grid.devices // 4
    ctx_ref, lse_ref, normed_ref, inv_ref, hid_ref, w, sems = rest[-7:]
    turn = pl.program_id(0)

    @pl.when(turn == 0)
    def _():
        start_natural(grid, me_ref, pieces, w, sems, 3 * quarter)

    live_len = len_ref[seq]
    length, pair = q_ref.shape
    half = pair // 2
    q, k, v = q_ref[...], k_ref[...], v_ref[...]
    lane = lax.broadcasted_iota(jnp.int32, (length, pair), 1)
    live = lax.broadcasted_iota(jnp.int32, (1, length), 1) < live_len
    outs, stats = [], []
    for h in (0, 1):
        mine = (lane >= half) if h else (lane < half)
        s = nt(jnp.where(mine, q, jnp.zeros_like(q)), k)
        s = jnp.where(live, s, masked_score)
        top = jnp.max(s, axis=-1, keepdims=True)
        p = jnp.exp(s - top)
        total = jnp.sum(p, axis=-1, keepdims=True)
        outs.append(nn(p.astype(BF), v) / total)
        stats.append(top + jnp.log(total))
    ctx = jnp.where(lane < half, outs[0], outs[1]).astype(BF)
    ctx_ref[:, pl.ds(pl.multiple_of(turn * pair, pair), pair)] = ctx
    turned = jnp.where(lane < half, stats[0], stats[1]).T
    lse_ref[0] = jnp.concatenate([turned[0:1], turned[half : half + 1]], axis=0)

    @pl.when(turn == pl.num_programs(0) - 1)
    def _():
        wait_natural(grid, pieces, w, sems, 3 * quarter, grid.devices, 3 * quarter)
        bo, _, _, g1, e1, _, _ = vector_refs(vec_ref, x_ref.shape[1])
        r = x_ref[...].astype(F32) + (nt(ctx_ref[...], w[...]) + bo)
        normed, inverse = norm_rows(r)
        normed_ref[...] = normed
        inv_ref[...] = inverse
        hid_ref[...] = (normed * g1 + e1).astype(BF)


def attend_call(grid, me, lens, qkv, x, vec, pieces, seqs, seq, before, deps):
    rows, width = x.shape
    length = rows // seqs
    pairs = H // 2
    pw = width // pairs
    at = lambda part: pl.BlockSpec((length, pw), lambda p: (seq, part * pairs + p))
    seq_rows = lambda w: pl.BlockSpec((length, w), lambda p: (seq, 0))
    first = 7 + len(pieces)
    return pl.pallas_call(
        lambda *r: attend_kernel(grid, len(pieces), seq, *r),
        grid=(pairs,),
        in_specs=[SMEM, SMEM, at(0), at(1), at(2), seq_rows(width), whole(vec.shape)]
        + [ANY] * (len(pieces) + len(before) + len(deps)),
        out_specs=[
            seq_rows(width),
            pl.BlockSpec((1, 2, length), lambda p: (seq * pairs + p, 0, 0)),
            seq_rows(width),
            seq_rows(1),
            seq_rows(width),
        ],
        out_shape=[
            jax.ShapeDtypeStruct((rows, width), BF),
            jax.ShapeDtypeStruct((seqs * pairs, 2, length), F32),
            jax.ShapeDtypeStruct((rows, width), F32),
            jax.ShapeDtypeStruct((rows, 1), F32),
            jax.ShapeDtypeStruct((rows, width), BF),
        ],
        scratch_shapes=[
            pltpu.VMEM((width, width), BF),
            pltpu.SemaphoreType.DMA((grid.devices,)),
        ],
        input_output_aliases={first + i: i for i in range(len(before))},
        compiler_params=params(),
        cost_estimate=cost(8 * H * length * length * (width // H), 9 << 20, H * length * length),
        name="attend",
    )(lens, me, qkv, qkv, qkv, x, vec, *pieces, *before, *deps)


PARTS = 4


def ffn_kernel(grid, per, me_ref, vec_ref, inv_ref, h_hbm, normed_hbm, dy_mine, dy_others, *rest):
    npieces = len(rest) - 24
    pieces = rest[:npieces]
    (out_mine, out_others, dres_hbm, datt_hbm, sums_ref, db1_ref, keep_hbm, send_hbm) = rest[
        npieces : npieces + 8
    ]
    (w, h, normed, dy, act, gp, acc, dres, dbr, out, dpre, stage, wsem, isem, osem, dsem) = rest[
        npieces + 8 :
    ]
    rows, width = h.shape
    units = w.shape[0] // 2
    size = units // PARTS
    tiles = rows // TILE
    me = me_ref[0]
    core = me & 1

    _, b1, b2, g1, e1, g2, e2 = vector_refs(vec_ref, width)
    loads = [
        pltpu.make_async_copy(src, dst, isem.at[i])
        for i, (src, dst) in enumerate(((h_hbm, h), (normed_hbm, normed)))
    ]
    loads[0].start()
    start_natural(grid, me_ref, pieces, w, wsem)
    loads[1].start()
    loads += load_sequences(core, dy_mine, dy_others, dy, dsem)
    loads[0].wait()
    half = grid.devices // 2

    def tile(r):
        return pl.ds(pl.multiple_of(r * TILE, TILE), TILE)

    for part in range(PARTS):
        for base in (0, half):
            wait_natural(
                grid, pieces, w, wsem, base + part * half // PARTS, base + (part + 1) * half // PARTS
            )
        up = slice(part * size, (part + 1) * size)
        down = slice(units + part * size, units + (part + 1) * size)

        @pl.loop(0, tiles)
        def _(r):
            at = tile(r)
            a, slope = gelu_pair(nt(h[at, :], w[up, :]) + b1[:, up])
            a = a.astype(BF)
            act[at, up] = a
            gp[at, up] = slope.astype(BF)
            more = nn(a, w[down, :])
            if part == 0:
                acc[at, :] = more
            else:
                acc[at, :] += more

    for copy in loads[1:]:
        copy.wait()
    sums_ref[...] = jnp.zeros_like(sums_ref)

    @pl.loop(0, tiles)
    def _(r):
        at = tile(r)
        hidden = normed[at, :] * g1 + e1
        value = hidden + (acc[at, :] + b2)
        n, inverse = norm_rows(value)
        out[at, :] = (n * g2 + e2).astype(BF)
        up = dy[at, :].astype(F32)
        d = norm_back(up, n, inverse, g2)
        low = d.astype(BF)
        dres[at, :] = d
        dbr[at, :] = low
        sums_ref[0:1] += jnp.sum(up * n, axis=0, keepdims=True)
        sums_ref[1:2] += jnp.sum(up, axis=0, keepdims=True)
        sums_ref[2:3] += jnp.sum(low.astype(F32), axis=0, keepdims=True)

    out_copies = store_sequences(core, out, out_mine, out_others, dsem)

    path = is_path(grid, per)
    blocks = size // per
    pending = [[], []]

    def emit(part, side, value):
        slot = part % 2
        stage[slot, side] = value
        if not path:
            copy = pltpu.make_async_copy(
                stage.at[slot, side],
                keep_hbm.at[pl.ds(side * units + part * size, size)],
                osem.at[slot, side, 0],
            )
            copy.start()
            pending[slot].append(copy)
            return
        for b in range(0, blocks, 2):
            for other, ref in ((0, keep_hbm), (1, send_hbm)):
                here = b + (core ^ other)
                block = side * half + part * blocks + here
                _, place = slot_of(grid, me ^ block, core)
                copy = pltpu.make_async_copy(
                    stage.at[slot, side, pl.ds(pl.multiple_of(here * per, per), per)],
                    ref.at[place],
                    osem.at[slot, side, b + other],
                )
                copy.start()
                pending[slot].append(copy)

    for part in range(PARTS):
        up = slice(part * size, (part + 1) * size)
        down = slice(units + part * size, units + (part + 1) * size)

        db1_ref[:, up] = jnp.zeros((1, size), F32)

        @pl.loop(0, tiles)
        def _(r):
            at = tile(r)
            d = (nt(dbr[at, :], w[down, :]) * gp[at, up].astype(F32)).astype(BF)
            dpre[at, :] = d
            db1_ref[:, up] += jnp.sum(d.astype(F32), axis=0, keepdims=True)
            more = nn(d, w[up, :])
            if part == 0:
                acc[at, :] = more
            else:
                acc[at, :] += more

        for copy in pending[part % 2]:
            copy.wait()
        pending[part % 2] = []
        emit(part, 0, tn(dpre[...], h[...]).astype(BF))
        emit(part, 1, tn(act[:, up], dbr[...]).astype(BF))

    for copy in out_copies:
        copy.wait()

    @pl.loop(0, tiles)
    def _(r):
        at = tile(r)
        dhid = dres[at, :] + acc[at, :]
        n = normed[at, :]
        d = norm_back(dhid, n, inv_ref[at, :], g1)
        low = d.astype(BF)
        dres[at, :] = d
        out[at, :] = low
        sums_ref[3:4] += jnp.sum(dhid * n, axis=0, keepdims=True)
        sums_ref[4:5] += jnp.sum(dhid, axis=0, keepdims=True)
        sums_ref[5:6] += jnp.sum(low.astype(F32), axis=0, keepdims=True)

    stores = [
        pltpu.make_async_copy(dres, dres_hbm, isem.at[1]),
        pltpu.make_async_copy(out, datt_hbm, isem.at[2]),
    ]
    for copy in stores:
        copy.start()
    for copy in stores + pending[0] + pending[1]:
        copy.wait()


def ffn_call(grid, me, vec, inv, h, normed, dy_mine, dy_others, pieces, per):
    rows, width = h.shape
    total = grid.devices * per
    units = total // 2
    size = units // PARTS
    paths = path_shapes(grid, grid.devices, per, width)
    return pl.pallas_call(
        lambda *r: ffn_kernel(grid, per, *r),
        in_specs=[SMEM, VMEM, VMEM, ANY, ANY, ANY, ANY] + [ANY] * len(pieces),
        out_specs=[ANY, ANY, ANY, ANY, VMEM, VMEM, ANY, ANY],
        out_shape=[
            jax.ShapeDtypeStruct(dy_mine.shape, BF),
            jax.ShapeDtypeStruct((dy_mine.shape[0] // 2,) + dy_mine.shape[1:], BF),
            jax.ShapeDtypeStruct((rows, width), F32),
            jax.ShapeDtypeStruct((rows, width), BF),
            jax.ShapeDtypeStruct((8, width), F32),
            jax.ShapeDtypeStruct((1, units), F32),
        ]
        + paths,
        scratch_shapes=[
            pltpu.VMEM((total, width), BF),
            pltpu.VMEM((rows, width), BF),
            pltpu.VMEM((rows, width), F32),
            pltpu.VMEM((rows, width), BF),
            pltpu.VMEM((rows, units), BF),
            pltpu.VMEM((rows, units), BF),
            pltpu.VMEM((rows, width), F32),
            pltpu.VMEM((rows, width), F32),
            pltpu.VMEM((rows, width), BF),
            pltpu.VMEM((rows, width), BF),
            pltpu.VMEM((rows, size), BF),
            pltpu.VMEM((2, 2, size, width), BF),
            pltpu.SemaphoreType.DMA((grid.devices,)),
            pltpu.SemaphoreType.DMA((3,)),
            pltpu.SemaphoreType.DMA((2, 2, max(size // per, 2))),
            pltpu.SemaphoreType.DMA((dy_mine.shape[0],)),
        ],
        compiler_params=params(),
        cost_estimate=cost(6 * rows * width * units, 40 << 20, 2 * rows * units),
        name="ffn",
    )(me, vec, inv, h, normed, dy_mine, dy_others, *pieces)


def out_back_kernel(grid, me_ref, datt_ref, ctx_ref, *rest):
    pieces, (dctx_ref, grad_ref, _, w, sems) = rest[:-6], rest[-5:]

    @pl.when(pl.program_id(0) == 0)
    def _():
        start_natural(grid, me_ref, pieces, w, sems, 3 * grid.devices // 4)
        grad_ref[...] = jnp.zeros_like(grad_ref)

    datt = datt_ref[...]
    grad_ref[...] += tn(datt, ctx_ref[...])

    @pl.when(pl.program_id(0) == 0)
    def _():
        first = 3 * grid.devices // 4
        wait_natural(grid, pieces, w, sems, first, grid.devices, first)

    dctx_ref[...] = nn(datt, w[...]).astype(BF)


def out_back_call(grid, me, datt, ctx, pieces, carry):
    rows, width = ctx.shape
    return pl.pallas_call(
        lambda *r: out_back_kernel(grid, *r),
        grid=(rows // TILE,),
        in_specs=[SMEM, rows_spec(width), rows_spec(width)] + [ANY] * (len(pieces) + 1),
        out_specs=[rows_spec(width), fixed(width, width), ANY],
        out_shape=[
            jax.ShapeDtypeStruct((rows, width), BF),
            jax.ShapeDtypeStruct((width, width), F32),
            jax.ShapeDtypeStruct(carry.shape, carry.dtype),
        ],
        input_output_aliases={3 + len(pieces): 2},
        scratch_shapes=[
            pltpu.VMEM((width, width), BF),
            pltpu.SemaphoreType.DMA((grid.devices,)),
        ],
        compiler_params=params(),
        cost_estimate=cost(2 * rows * width * width, 12 << 20),
        name="out_back",
    )(me, datt, ctx, *pieces, carry)


def attend_back_kernel(seq, len_ref, q_ref, k_ref, v_ref, d_ref, lse_ref, *rest):
    dz_ref, db_ref, _ = rest[-3:]
    live_len = len_ref[seq]
    length, pair = q_ref.shape
    half = pair // 2
    q, k, v, d = q_ref[...], k_ref[...], v_ref[...], d_ref[...]
    lane = lax.broadcasted_iota(jnp.int32, (length, pair), 1)
    live = lax.broadcasted_iota(jnp.int32, (length, 1), 0) < live_len
    zero = jnp.zeros_like(q)
    dq = dk = dv = None
    for h in (0, 1):
        mine = (lane >= half) if h else (lane < half)
        qh, kh, dh = (jnp.where(mine, t, zero) for t in (q, k, d))
        s = nt(k, qh)
        p = jnp.where(live, jnp.exp(s - lse_ref[0, h : h + 1, :]), 0.0)
        dp = nt(v, dh)
        inner = jnp.sum(p * dp, axis=0, keepdims=True)
        ds = (p * (dp - inner)).astype(BF)
        a = nn(p.astype(BF), dh)
        b = nn(ds, qh)
        c = tn(ds, kh)
        dv = a if dv is None else dv + a
        dk = b if dk is None else dk + b
        dq = c if dq is None else dq + c
    scale = half ** -0.5
    dq = (dq.astype(BF).astype(F32) * scale).astype(BF)
    dv = dv.astype(BF)
    dz_ref[0] = dq
    dz_ref[1] = dk.astype(BF)
    dz_ref[2] = dv
    db_ref[0:1] = jnp.sum(dq.astype(F32), axis=0, keepdims=True)
    db_ref[1:2] = jnp.sum(dv.astype(F32), axis=0, keepdims=True)


def attend_back_call(lens, qkv, dctx, lse, seqs, seq, dz, carry, deps):
    rows, width = dctx.shape
    length = rows // seqs
    pairs = H // 2
    pw = width // pairs
    at = lambda part: pl.BlockSpec((length, pw), lambda p: (seq, part * pairs + p))
    more = [carry] + ([] if dz is None else [dz]) + list(deps)
    return pl.pallas_call(
        lambda *r: attend_back_kernel(seq, *r),
        grid=(pairs,),
        in_specs=[
            SMEM,
            at(0),
            at(1),
            at(2),
            at(0),
            pl.BlockSpec((1, 2, length), lambda p: (seq * pairs + p, 0, 0)),
        ]
        + [ANY] * len(more),
        out_specs=[
            pl.BlockSpec((3, length, pw), lambda p: (0, seq, p)),
            pl.BlockSpec((2, pw), lambda p: (0, p)),
            ANY,
        ],
        out_shape=[
            jax.ShapeDtypeStruct((3, rows, width), BF),
            jax.ShapeDtypeStruct((2, width), F32),
            jax.ShapeDtypeStruct(carry.shape, carry.dtype),
        ],
        input_output_aliases={6: 2} if dz is None else {6: 2, 7: 0},
        compiler_params=params(),
        cost_estimate=cost(
            20 * H * length * length * (width // H), 6 << 20, H * length * length
        ),
        name="attend_back",
    )(lens, qkv, qkv, qkv, dctx, lse, *more)


def attn_grad_kernel(grid, per, me_ref, dz_ref, x_ref, gout_ref, sums, db1, db_a, db_b, *rest):
    keep_ref, send_ref, total, line, gvec = rest[-5:]
    part = pl.program_id(0)
    width = x_ref.shape[1]
    total[pl.ds(pl.multiple_of(part * width, width), width), :] = tn(dz_ref[0], x_ref[...])

    @pl.when(part == 2)
    def _():
        total[3 * width :, :] = gout_ref[...]
        db = db_a[...] + db_b[...]
        tail = 3 * width + FF
        line[:, 0:width] = db[0:1]
        line[:, width : 2 * width] = db[1:2]
        line[:, 2 * width : 3 * width] = sums[5:6]
        line[:, 3 * width : tail] = db1[...]
        for i, row in enumerate((2, 3, 4, 0, 1)):
            line[:, tail + i * width : tail + (i + 1) * width] = sums[row : row + 1]
        count = line.shape[1] // grid.devices
        gvec[...] = jnp.zeros_like(gvec)
        for d in range(grid.devices):
            gvec[d, 0:1, 0:count] = line[:, d * count : (d + 1) * count]
        if not is_path(grid, per):
            keep_ref[...] = total[...].astype(BF)
            send_ref[...] = gvec[...].astype(BF)
            return
        me = me_ref[0]
        core = me & 1
        at = 0
        for i3 in range(grid.side):
            for i2 in range(grid.side):
                for iz in range(grid.nz):
                    for other, ref in ((0, keep_ref), (1, send_ref)):
                        block = me ^ grid.label(core ^ other, other, i3, i2, iz)
                        start = pl.multiple_of(block * per, per)
                        ref[at, 0:per] = total[pl.ds(start, per), :].astype(BF)
                        ref[at, per : per + 8] = gvec[block].astype(BF)
                    at += 1


def attn_grad_call(grid, me, dz, x, gout, vectors, per, deps):
    rows, width = x.shape
    paths = path_shapes(grid, grid.devices, per, width)
    if is_path(grid, per):
        paths = [jax.ShapeDtypeStruct((p.shape[0], per + 8, width), BF) for p in paths]
    return pl.pallas_call(
        lambda *r: attn_grad_kernel(grid, per, *r),
        grid=(3,),
        in_specs=[
            SMEM,
            pl.BlockSpec((1, rows, width), lambda i: (i, 0, 0)),
            fixed(rows, width),
            fixed(width, width),
        ]
        + [fixed(*v.shape) for v in vectors]
        + [ANY] * len(deps),
        out_specs=[whole(p.shape) for p in paths],
        out_shape=paths,
        scratch_shapes=[
            pltpu.VMEM((4 * width, width), F32),
            pltpu.VMEM((1, 8 * width + FF), F32),
            pltpu.VMEM((grid.devices, 8, width), F32),
        ],
        compiler_params=params(),
        cost_estimate=cost(3 * rows * width * width, 16 << 20),
        name="attn_grad",
    )(me, dz, x, gout, *vectors, *deps)


def input_grad_kernel(grid, me_ref, dz_hbm, dres_hbm, *rest):
    pieces, (mine, others, _, dz, total, w, sems, isem, osem) = rest[:-10], rest[-9:]
    rows, width = total.shape
    blocks = grid.devices // 4
    core = me_ref[0] & 1
    loads = [
        pltpu.make_async_copy(dz_hbm.at[part], dz.at[part], isem.at[part]) for part in range(3)
    ] + [pltpu.make_async_copy(dres_hbm, total, isem.at[3])]
    loads[3].start()
    loads[0].start()
    start_natural(grid, me_ref, pieces, w, sems, 0, 3 * blocks)
    loads[1].start()
    loads[2].start()
    loads[3].wait()
    for part in range(3):
        loads[part].wait()
        wait_natural(grid, pieces, w, sems, part * blocks, (part + 1) * blocks, 0, 3 * blocks)

        @pl.loop(0, rows // TILE)
        def _(r):
            at = pl.ds(pl.multiple_of(r * TILE, TILE), TILE)
            total[at, :] += nn(dz[part, at, :], w[part * width : (part + 1) * width, :])

    for copy in store_sequences(core, total, mine, others, osem):
        copy.wait()


def input_grad_call(grid, me, dz, dres, pieces, shape, carry):
    rows, width = dres.shape
    return pl.pallas_call(
        lambda *r: input_grad_kernel(grid, *r),
        in_specs=[SMEM, ANY, ANY] + [ANY] * (len(pieces) + 1),
        out_specs=[ANY, ANY, ANY],
        out_shape=[
            jax.ShapeDtypeStruct(shape, F32),
            jax.ShapeDtypeStruct((shape[0] // 2,) + shape[1:], F32),
            jax.ShapeDtypeStruct(carry.shape, carry.dtype),
        ],
        input_output_aliases={3 + len(pieces): 2},
        scratch_shapes=[
            pltpu.VMEM((3, rows, width), BF),
            pltpu.VMEM((rows, width), F32),
            pltpu.VMEM((3 * width, width), BF),
            pltpu.SemaphoreType.DMA((grid.devices,)),
            pltpu.SemaphoreType.DMA((4,)),
            pltpu.SemaphoreType.DMA((shape[0],)),
        ],
        compiler_params=params(),
        cost_estimate=cost(3 * rows * width * width, 16 << 20),
        name="input_grad",
    )(me, dz, dres, *pieces, carry)


def gate(value, deps):
    return pl.pallas_call(
        lambda *r: None,
        in_specs=[ANY] * (1 + len(deps)),
        out_specs=ANY,
        out_shape=jax.ShapeDtypeStruct(value.shape, value.dtype),
        input_output_aliases={0: 0},
        compiler_params=params(),
        cost_estimate=cost(0, 0),
        name="gate",
    )(value, *deps)


def ordered_block_kernel(w_ref, *rest):
    rest[-1][...] = w_ref[...].T.astype(BF)


def ordered_block(weights, deps):
    width, per = weights.shape
    return pl.pallas_call(
        ordered_block_kernel,
        in_specs=[VMEM] + [ANY] * len(deps),
        out_specs=VMEM,
        out_shape=jax.ShapeDtypeStruct((per, width), BF),
        compiler_params=params(),
        name="ordered_block",
    )(weights, *deps)


def ordered_stack_kernel(count, *rest):
    for i in range(count):
        rest[-1][i] = rest[i][...]


def ordered_stack(parts, deps):
    return pl.pallas_call(
        lambda *r: ordered_stack_kernel(len(parts), *r),
        in_specs=[VMEM] * len(parts) + [ANY] * len(deps),
        out_specs=VMEM,
        out_shape=jax.ShapeDtypeStruct((len(parts),) + parts[0].shape, parts[0].dtype),
        compiler_params=params(),
        name="ordered_stack",
    )(*parts, *deps)


def adam_update(master, moment, second, grad, rate):
    moment_new = decay_rate * moment + (1.0 - decay_rate) * grad
    second_new = decay_rate * second + (1.0 - decay_rate) * grad * grad
    correction = 1.0 - decay_rate**STEP
    direction = moment_new / correction / (jnp.sqrt(second_new / correction) + adam_epsilon)
    master_new = master - rate * (direction + weight_decay * master)
    return (moment_new, second_new, master_new)


def join_sequences(mine, others, core):
    count = others.shape[0]
    return lax.dynamic_update_slice(mine, others, ((1 - core) * count, 0, 0))


def local(
    tokens,
    cotangent,
    seq_lengths,
    slot_order,
    attn_weights,
    attn_moment,
    attn_second,
    ffn_weights,
    ffn_moment,
    ffn_second,
    vectors,
    vector_moment,
    vector_second,
):
    grid = Grid(lax.axis_size("dp"))
    core = lax.axis_index("seq")
    shard_index = lax.axis_index(AXES)
    me = shard_index.astype(jnp.int32).reshape(1)
    seq_count, half_len, width = tokens.shape
    seqs = seq_count // 2
    length = 2 * half_len
    rows = seqs * length
    per, ffn_per = attn_weights.shape[1], ffn_weights.shape[1]
    vec_per = vectors.shape[0]
    path = is_path(grid, per) and is_path(grid, ffn_per)

    slot_pick = (slot_order[0][:, None] == jnp.arange(seq_count)[None, :]).astype(jnp.int32)
    slot_len = jnp.sum(slot_pick * seq_lengths[0][None, :], axis=1)
    lens = lax.dynamic_slice_in_dim(slot_len, core * seqs, seqs, 0)

    vec_rows = jnp.zeros((8, width), BF)
    vec_rows = lax.dynamic_update_slice(vec_rows, vectors.astype(BF)[None, :], (0, 0))
    attn_block = jnp.concatenate([attn_weights.astype(BF).T, vec_rows])
    ffn_block = ffn_weights.astype(BF).T

    other_core = lambda value: permute(value, grid, lambda c: 1)
    tokens_other = other_core(tokens)
    if path:
        attn_parts = gather_z(grid, attn_block)
        ffn_block = ordered_block(ffn_weights, attn_parts[1:2])
        ffn_parts = gather_z(grid, ffn_block)
        attn_z = jnp.stack(attn_parts)
        attn_two = gather_two(grid, attn_z)
        attn_three = gather_three(grid, attn_two)
        ffn_z = ordered_stack(ffn_parts, attn_three[-1:])
        ffn_two = gather_two(grid, ffn_z)
        weights = with_core(grid, attn_two + attn_three)
        vec = natural_vectors(grid, weights, core, me[0], per, vec_per)
    else:
        whole_rows = lambda block: [lax.all_gather(block, AXES, axis=0, tiled=True)]
        weights = whole_rows(attn_block[:per])
        ffn_pieces = whole_rows(ordered_block(ffn_weights, []))
        ffn_two = []
        vec = lax.all_gather(attn_block[per:], AXES)[:, 0, :vec_per].reshape(1, -1).astype(F32)
    dy_other = other_core(cotangent)

    qkv, x = qkv_call(grid, me, vec, tokens, tokens_other, weights)
    fwd = attend_call(grid, me, lens, qkv, x, vec, weights, seqs, 0, [], [])
    ffn_two = ffn_two[:1] + [gate(t, fwd[:1]) for t in ffn_two[1:]]
    fwd = attend_call(grid, me, lens, qkv, x, vec, weights, seqs, 1, fwd, ffn_two[1:])
    ctx, lse, normed, inv, hidden = fwd
    if path:
        ffn_three = gather_three(grid, ffn_two)
        ffn_three = ffn_three[:1] + [gate(t, fwd[:1]) for t in ffn_three[1:]]
        ffn_pieces = with_core(grid, ffn_two + ffn_three)
    out, out_other, dres_one, datt, sums, db1, keep_f, send_f = ffn_call(
        grid, me, vec, inv, hidden, normed, cotangent, dy_other, ffn_pieces, ffn_per
    )
    layer_out = join_sequences(out, other_core(out_other), core)

    sums_f = Sums(grid, path, keep_f, send_f)
    dctx, gout, sums_f.keep = out_back_call(grid, me, datt, ctx, weights, sums_f.keep)
    sends = sums_f.add_core()
    dz, db_a, sums_f.keep = attend_back_call(
        lens, qkv, dctx, lse, seqs, 0, None, sums_f.keep, sends
    )
    sends = sums_f.add_three()
    dz, db_b, sums_f.keep = attend_back_call(
        lens, qkv, dctx, lse, seqs, 1, dz, sums_f.keep, sends
    )
    sends = sums_f.add_two()
    keep_c, send_c = attn_grad_call(
        grid, me, dz, x, gout, [sums, db1, db_a, db_b], per, sends
    )
    sums_c = Sums(grid, path, keep_c, send_c)
    sums_c.add_core()
    dx, dx_other, sums_c.keep = input_grad_call(
        grid, me, dz, dres_one, weights, tokens.shape, sums_c.keep
    )
    sums_c.add_three()
    input_grad = join_sequences(dx, other_core(dx_other), core)
    sums_c.add_two()
    ffn_sum = sums_f.add_z()
    attn_sum = sums_c.add_z()

    vector_sum = attn_sum[per, :vec_per]
    attn_sum = attn_sum[:per].T
    ffn_sum = ffn_sum[:ffn_per].T

    attn_cols = shard_index * per + jnp.arange(per)
    attn_rate = jnp.where(
        attn_cols < 2 * width, math.sqrt(2.0), jnp.where(attn_cols < 3 * width, 1.5, 1.8)
    ) * width ** (-0.5)
    ffn_cols = shard_index * ffn_per + jnp.arange(ffn_per)
    ffn_rate = jnp.where(ffn_cols < FF, width ** (-0.5), 1.5 * FF ** (-0.5))
    attn_m, attn_v, attn_new = adam_update(
        attn_weights, attn_moment, attn_second, attn_sum, attn_rate[None, :]
    )
    ffn_m, ffn_v, ffn_new = adam_update(
        ffn_weights, ffn_moment, ffn_second, ffn_sum, ffn_rate[None, :]
    )
    vec_m, vec_v, vec_new = adam_update(
        vectors, vector_moment, vector_second, vector_sum, vector_rate
    )
    return (
        layer_out,
        input_grad,
        attn_m,
        attn_v,
        attn_new,
        attn_new.astype(BF),
        ffn_m,
        ffn_v,
        ffn_new,
        ffn_new.astype(BF),
        vec_m,
        vec_v,
        vec_new,
        vec_new.astype(BF),
    )


def solution(mesh):
    columns = P(None, AXES)
    flat = P(AXES)
    rows = P("dp", "seq", None)
    placed = (rows, rows, P("dp", None), P("dp", None)) + (columns,) * 6 + (flat,) * 3
    return jax.shard_map(
        local,
        mesh=mesh,
        in_specs=placed,
        out_specs=(rows, rows) + (columns,) * 8 + (flat,) * 4,
        check_vma=False,
    )
```

time: 759 us -> 316 us (0.42); the launches traced: 748 us -> 313 us
  waiting for transfers between devices: 242 us -> 66.2 us
  matrix products: 172 us -> 0 us
  Pallas kernels: 0 us -> 162 us
  blocking collectives: 113 us -> 0 us
  local copies, waits for them, and re-layouts: 122 us -> 13.5 us
  other arithmetic: 83.3 us -> 23.7 us
  starting transfers between devices: 0.16 us -> 46.5 us
  between operations: 15 us -> 1.54 us
    unnamed x5 -> x0, waiting for transfers between devices: 211 us -> none
    dot_general x40 -> x0, matrix products: 172 us -> none  [the longest x1 36.9 us: local(): jnp.dot(hidden_low, up_weight, preferred_element_type=jnp.float32) + up_bias]
    pallas_call x0 -> x13, Pallas kernels: none -> 162 us  [the longest x1 63.1 us: ffn_call(): pl.pallas_call(lambda *r: ffn_kernel(grid, per, *r), in_specs=[SMEM, VMEM...]
    unnamed x2 -> x0, blocking collectives: 82.9 us -> none
    ppermute x0 -> x38, waiting for transfers between devices: none -> 66.2 us  [permute(): return lax.ppermute(value, AXES, pairs)]
    ppermute x0 -> x38, starting transfers between devices: none -> 46.5 us  [permute(): return lax.ppermute(value, AXES, pairs)]
    convert_element_type x3 -> x1, local copies, waits for them, and re-layouts: 34.8 us -> 0.73 us  [natural_vectors(): return value.reshape(1, -1).astype(F32)]
    all_to_all x4 -> x0, blocking collectives: 30.4 us -> none  [the longest x1 9.17 us: local(): lax.all_to_all(grad_heads.reshape(seq_count, full_len, 3, 1, head_width),...]
  transfers between devices with their start and end apart: 4 -> 38, of which waited for: 3 -> 17; matrix products, arithmetic and copies ran while one was open for 23% -> 6% of each run, Pallas kernels for 0% -> 28%
where the time goes in v1:
time: 316 us; the launch traced here: 313 us
  Pallas kernels  162 us (51%)
  waiting for transfers between devices  66.2 us (21%)
  starting transfers between devices  46.5 us (15%)
  other arithmetic  23.7 us (8%)
  local copies, waits for them, and re-layouts  13.5 us (4%)
    ppermute x38, waiting for transfers between devices, permute(): return lax.ppermute(value, AXES, pairs)  66.2 us
    pallas_call x1, Pallas kernels, ffn_call(): pl.pallas_call(lambda *r: ffn_kernel(grid, per, *r), in_specs=[SMEM, VMEM...  63.1 us
    ppermute x38, starting transfers between devices, permute(): return lax.ppermute(value, AXES, pairs)  46.5 us
    pallas_call x2, Pallas kernels, attend_back_call(): pl.pallas_call(lambda *r: attend_back_kernel(seq, *r), grid=(pairs,), in_...  30.1 us
    pallas_call x2, Pallas kernels, attend_call(): pl.pallas_call(lambda *r: attend_kernel(grid, len(pieces), seq, *r), grid...  23.7 us
    pallas_call x1, Pallas kernels, input_grad_call(): pl.pallas_call(lambda *r: input_grad_kernel(grid, *r), in_specs=[SMEM, AN...  11.3 us
    pallas_call x1, Pallas kernels, qkv_call(): pl.pallas_call(lambda *r: qkv_kernel(grid, *r), in_specs=[SMEM, VMEM, ANY...  11 us
    pallas_call x1, Pallas kernels, attn_grad_call(): pl.pallas_call(lambda *r: attn_grad_kernel(grid, per, *r), grid=(3,), in_...  10.2 us
  transfers between devices with their start and end apart: 38, of which 17 were waited for; matrix products, arithmetic and copies ran while one was open for 6% of the time, Pallas kernels for 28%

profile of v1, /device:TPU:0, one launch (start us, length us, event | category | flops | bytes accessed | tf_op | source)
XLA Modules:
  0.0 313.1 jit_solution(5781371595759175598)
XLA Ops:
  2.4 5.1 %collective-permute-start.2 = (bf16[104,768]{1,0:T(8,128)(2,1)S(1)}, bf16[104,768]{1,0:T(8,128)(2,1)S(1)}, u32[]{:S(2)}, u32[]{:S(2)}) collective-permute-start(bf16[104,768]{1,0:T(8,128)(2,1)S(1)} %get-tuple-element.121), channel_id=1, source_target_pairs={{0,24},{1,25},{2,26},{3,27},{4,28},{5,29},{6,30},{7,31},{8,16},{9,... | collective-permute-start | bytes 479240 | tf_op jit(solution)/shard_map/ppermute | solution.py:72
  8.2 4.4 %collective-permute-done.2 = bf16[104,768]{1,0:T(8,128)(2,1)S(1)} collective-permute-done((bf16[104,768]{1,0:T(8,128)(2,1)S(1)}, bf16[104,768]{1,0:T(8,128)(2,1)S(1)}, u32[]{:S(2)}, u32[]{:S(2)}) %collective-permute-start.2) | collective-permute-done | bytes 159776 | tf_op jit(solution)/shard_map/ppermute | solution.py:72
  12.6 8.5 %collective-permute-done.1 = bf16[104,768]{1,0:T(8,128)(2,1)S(1)} collective-permute-done((bf16[104,768]{1,0:T(8,128)(2,1)S(1)}, bf16[104,768]{1,0:T(8,128)(2,1)S(1)}, u32[]{:S(2)}, u32[]{:S(2)}) %collective-permute-start.1) | collective-permute-done | bytes 159776 | tf_op jit(solution)/shard_map/ppermute | solution.py:72
  21.2 1.6 collective-permute-start.3
  22.8 1.5 collective-permute-start.4
  25.4 2.0 ordered_block.1.r_0_
  28.2 3.0 collective-permute-start.12
  31.3 7.2 %collective-permute-done.3.r_5_.r_8_.r_4_ = bf16[4,104,768]{2,1,0:T(8,128)(2,1)S(1)} collective-permute-done((bf16[4,104,768]{2,1,0:T(8,128)(2,1)S(1)}, bf16[4,104,768]{2,1,0:T(8,128)(2,1)S(1)}, u32[]{:S(2)}, u32[]{:S(2)}) %collective-permute-start.3) | collective-permute-done | bytes 639008 | tf_op jit(solution)/shard_map/ppermute | solution.py:72
  38.6 3.8 %collective-permute-done.11.r_1_ = bf16[192,768]{1,0:T(8,128)(2,1)S(1)} collective-permute-done((bf16[192,768]{1,0:T(8,128)(2,1)}, bf16[192,768]{1,0:T(8,128)(2,1)S(1)}, u32[]{:S(2)}, u32[]{:S(2)}) %collective-permute-start.11) | collective-permute-done | bytes 294944 | tf_op jit(solution)/shard_map/ppermute | solution.py:72
  42.4 1.5 collective-permute-start.13
  44.4 1.2 collective-permute-done.12.r_2_
  45.6 7.5 %collective-permute-done.13.r_3_ = bf16[192,768]{1,0:T(8,128)(2,1)S(1)} collective-permute-done((bf16[192,768]{1,0:T(8,128)(2,1)}, bf16[192,768]{1,0:T(8,128)(2,1)S(1)}, u32[]{:S(2)}, u32[]{:S(2)}) %collective-permute-start.13) | collective-permute-done | bytes 294944 | tf_op jit(solution)/shard_map/ppermute | solution.py:72
  54.7 2.3 ordered_stack.1.r_7_
  63.3 11.0 %qkv.1 = (bf16[1024,2304]{1,0:T(8,128)(2,1)}, bf16[1024,768]{1,0:T(8,128)(2,1)}) custom-call(s32[1]{0:T(128)} %bitcast.r_0_.r_1_, f32[1,9216]{1,0:T(1,128)} %reshape.74.r_1_.r_6_, bf16[4,256,768]{2,1,0:T(8,128)(2,1)} %r_2_.1, bf16[4,256,768]{2,1,0:T(8,128)(2,1)} %collective-permute-done.10.r_3_, bf16[4,104,768]{2,1,0:T(8,128)(2,1)} %copy-done, ...), custom_call_target="tpu_custom_call" | custom-call | flops 226492416 | bytes 786432 | tf_op jit(solution)/shard_map/qkv/pallas_call | solution.py:372
  74.2 11.9 %attend.2 = (bf16[1024,768]{1,0:T(8,128)(2,1)}, f32[12,2,512]{2,1,0:T(2,128)}, f32[1024,768]{1,0:T(8,128)}, f32[1024,1]{1,0:T(8,128)}, bf16[1024,768]{1,0:T(8,128)(2,1)}) custom-call(s32[2]{0:T(128)} %dynamic_slice.3.r_0_, s32[1]{0:T(128)} %bitcast.r_0_.r_1_, bf16[1024,2304]{1,0:T(8,128)(2,1)} %get-tuple-element.48.r_2_.r_3_.r_4_.r_1_, ...), custom_call_target="tpu_custom_call" | custom-call | flops 201326592 | bytes 589824 | tf_op jit(solution)/shard_map/attend/pallas_call | solution.py:450
  86.2 1.6 collective-permute-start.17
  88.7 11.8 %attend.3 = (bf16[1024,768]{1,0:T(8,128)(2,1)}, f32[12,2,512]{2,1,0:T(2,128)}, f32[1024,768]{1,0:T(8,128)}, f32[1024,1]{1,0:T(8,128)}, bf16[1024,768]{1,0:T(8,128)(2,1)}) custom-call(s32[2]{0:T(128)} %dynamic_slice.3.r_0_, s32[1]{0:T(128)} %bitcast.r_0_.r_1_, ...), custom_call_target="tpu_custom_call", output_to_operand_aliasing={{0}: (15, {}), {1}: (16, {}), {2}: (17, {}), {3}: (18, {}),... | custom-call | flops 201326592 | bytes 589824 | tf_op jit(solution)/shard_map/attend/pallas_call | solution.py:450
  100.6 2.1 collective-permute-done.17.r_0_
  103.7 3.0 collective-permute-done.21.r_14_
  107.7 63.1 %ffn.1 = (bf16[4,256,768]{2,1,0:T(8,128)(2,1)}, bf16[2,256,768]{2,1,0:T(8,128)(2,1)}, f32[1024,768]{1,0:T(8,128)}, bf16[1024,768]{1,0:T(8,128)(2,1)}, f32[8,768]...) custom-call(s32[1]{0:T(128)} %bitcast.r_0_.r_1_, ...), custom_call_target="tpu_custom_call" | custom-call | flops 1811939328 | bytes 2621440 | tf_op jit(solution)/shard_map/ffn/pallas_call | solution.py:642
  171.0 7.9 %out_back.1 = (bf16[1024,768]{1,0:T(8,128)(2,1)}, f32[768,768]{1,0:T(8,128)}, bf16[16,192,768]{2,1,0:T(8,128)(2,1)}) custom-call(s32[1]{0:T(128)} %bitcast.r_0_.r_1_, bf16[1024,768]{1,0:T(8,128)(2,1)} %get-tuple-element.61.r_1_, bf16[1024,768]{1,0:T(8,128)(2,1)} %get-tuple-element.58.r_1_.r_2_, ...), custom_call_target="tpu_custom_call", output_to_operand_aliasing={{2}: (11, {})} | custom-call | flops 150994944 | bytes 786432 | tf_op jit(solution)/shard_map/out_back/pallas_call | solution.py:700
  179.0 3.9 %add_convert_fusion.1 = (bf16[4,192,768]{2,1,0:T(8,128)(2,1)S(1)}, bf16[4,192,768]{2,1,0:T(8,128)(2,1)S(1)}) fusion(bf16[16,192,768]{2,1,0:T(8,128)(2,1)S(1)} %collective-permute-done.23, bf16[16,192,768]{2,1,0:T(8,128)(2,1)} %get-tuple-element.65.r_6_), kind=kLoop, calls=%fused_computation.1 | loop fusion | flops 4718592 | bytes 7077888 | tf_op jit(solution)/shard_map/convert_element_type | solution.py:213
  182.9 1.6 collective-permute-start.24
  185.0 15.0 %attend_back.2 = (bf16[3,1024,768]{2,1,0:T(8,128)(2,1)}, f32[2,768]{1,0:T(2,128)}, bf16[16,192,768]{2,1,0:T(8,128)(2,1)}) custom-call(s32[2]{0:T(128)} %dynamic_slice.3.r_0_, bf16[1024,2304]{1,0:T(8,128)(2,1)} %get-tuple-element.48.r_2_.r_3_.r_4_.r_1_, bf16[1024,2304]{1,0:T(8,128)(2,1)} %get-tuple-element.48.r_2_.r_3_.r_4_.r_1_, ...), custom_call_target="tpu_custom_call", output_to_operand_aliasing={{2}: (6, {})} | custom-call | flops 503316480 | bytes 393216 | tf_op jit(solution)/shard_map/attend_back/pallas_call | solution.py:762
  200.1 2.1 add_convert_fusion.r_8_
  202.1 1.6 collective-permute-start.26
  203.7 15.1 %attend_back.3 = (bf16[3,1024,768]{2,1,0:T(8,128)(2,1)}, f32[2,768]{1,0:T(2,128)}, bf16[16,192,768]{2,1,0:T(8,128)(2,1)}) custom-call(s32[2]{0:T(128)} %dynamic_slice.3.r_0_, bf16[1024,2304]{1,0:T(8,128)(2,1)} %get-tuple-element.48.r_2_.r_3_.r_4_.r_1_, ...), custom_call_target="tpu_custom_call", output_to_operand_aliasing={{2}: (6, {}), {0}: (7, {})} | custom-call | flops 503316480 | bytes 393216 | tf_op jit(solution)/shard_map/attend_back/pallas_call | solution.py:762
  219.2 4.8 %collective-permute-done.26 = bf16[4,192,768]{2,1,0:T(8,128)(2,1)} collective-permute-done((bf16[4,192,768]{2,1,0:T(8,128)(2,1)S(1)}, bf16[4,192,768]{2,1,0:T(8,128)(2,1)}, u32[]{:S(2)}, u32[]{:S(2)}) %collective-permute-start.26) | collective-permute-done | bytes 1179680 | tf_op jit(solution)/shard_map/ppermute | solution.py:72
  223.9 2.9 fusion.9
  226.8 10.2 %attn_grad.1 = (bf16[16,104,768]{2,1,0:T(8,128)(2,1)}, bf16[16,104,768]{2,1,0:T(8,128)(2,1)}) custom-call(s32[1]{0:T(128)} %bitcast.r_0_.r_1_, bf16[3,1024,768]{2,1,0:T(8,128)(2,1)} %get-tuple-element.69.r_1_, bf16[1024,768]{1,0:T(8,128)(2,1)} %get-tuple-element.49.r_5_.r_2_, f32[768,768]{1,0:T(8,128)} %get-tuple-element.71.r_3_, ...), custom_call_target="tpu_custom_call" | custom-call | flops 226492416 | bytes 1048576 | tf_op jit(solution)/shard_map/attn_grad/pallas_call | solution.py:837
  237.6 4.7 %collective-permute-done.28 = bf16[16,104,768]{2,1,0:T(8,128)(2,1)S(1)} collective-permute-done((bf16[16,104,768]{2,1,0:T(8,128)(2,1)}, bf16[16,104,768]{2,1,0:T(8,128)(2,1)S(1)}, u32[]{:S(2)}, u32[]{:S(2)}) %collective-permute-start.28) | collective-permute-done | bytes 2555936 | tf_op jit(solution)/shard_map/ppermute | solution.py:72
  242.3 2.5 add_convert_fusion.5
  244.8 1.5 collective-permute-start.30
  246.3 1.5 collective-permute-start.29
  247.8 11.3 %input_grad.1 = (f32[4,256,768]{2,1,0:T(8,128)}, f32[2,256,768]{2,1,0:T(8,128)}, bf16[16,104,768]{2,1,0:T(8,128)(2,1)}) custom-call(s32[1]{0:T(128)} %bitcast.r_0_.r_1_, bf16[3,1024,768]{2,1,0:T(8,128)(2,1)} %get-tuple-element.69.r_1_, f32[1024,768]{1,0:T(8,128)} %get-tuple-element.70.r_2_, ...), custom_call_target="tpu_custom_call", output_to_operand_aliasing={{2}: (11, {})} | custom-call | flops 226492416 | bytes 1048576 | tf_op jit(solution)/shard_map/input_grad/pallas_call | solution.py:890
  259.1 2.2 add_convert_fusion.3
  261.9 2.1 collective-permute-start.37
  264.0 4.9 %collective-permute-start.36 = (bf16[192,768]{1,0:T(8,128)(2,1)}, bf16[192,768]{1,0:T(8,128)(2,1)S(1)}, u32[]{:S(2)}, u32[]{:S(2)}) collective-permute-start(bf16[192,768]{1,0:T(8,128)(2,1)} %get-tuple-element.111.r_9_), channel_id=1, source_target_pairs={{0,16},{1,17},{2,18},{3,19},{4,20},{5,21},{6,22},{7,23},{8,24},{9,... | collective-permute-start | bytes 884744 | tf_op jit(solution)/shard_map/ppermute | solution.py:72
  268.9 2.1 constant_dynamic-update-slice_fusion.8
  272.0 1.7 fusion.11
  273.7 2.1 collective-permute-start.34
  275.8 11.9 %collective-permute-start.33 = (bf16[104,768]{1,0:T(8,128)(2,1)S(1)}, bf16[104,768]{1,0:T(8,128)(2,1)S(1)}, u32[]{:S(2)}, u32[]{:S(2)}) collective-permute-start(bf16[104,768]{1,0:T(8,128)(2,1)S(1)} %get-tuple-element.117), channel_id=1, source_target_pairs={{0,16},{1,17},{2,18},{3,19},{4,20},{5,21},{6,22},{7,23},{8,24},{9,... | collective-permute-start | bytes 479240 | tf_op jit(solution)/shard_map/ppermute | solution.py:72
  287.7 10.9 %collective-permute-done.36 = bf16[192,768]{1,0:T(8,128)(2,1)S(1)} collective-permute-done((bf16[192,768]{1,0:T(8,128)(2,1)}, bf16[192,768]{1,0:T(8,128)(2,1)S(1)}, u32[]{:S(2)}, u32[]{:S(2)}) %collective-permute-start.36) | collective-permute-done | bytes 294944 | tf_op jit(solution)/shard_map/ppermute | solution.py:72
  298.7 3.3 %fusion.21 = (bf16[768,192]{0,1:T(8,128)(2,1)}, f32[768,192]{0,1:T(8,128)}, f32[768,192]{0,1:T(8,128)}, f32[768,192]{0,1:T(8,128)}) fusion(f32[768,192]{0,1:T(8,128)S(1)} %copy-done.14, f32[192]{0:T(256)S(1)} %compare_select_fusion, f32[768,192]{0,1:T(8,128)S(1)} %copy-done.22, f32[768,192]{0,1:T(8,128)S(1)} %copy-done.23, ...), kind=kLoop, calls=%fused_computation.80 | loop fusion | flops 4128768 | bytes 5899008 | tf_op jit(solution)/shard_map/convert_element_type | solution.py:1098
  301.9 3.5 %collective-permute-done.33 = bf16[104,768]{1,0:T(8,128)(2,1)S(1)} collective-permute-done((bf16[104,768]{1,0:T(8,128)(2,1)S(1)}, bf16[104,768]{1,0:T(8,128)(2,1)S(1)}, u32[]{:S(2)}, u32[]{:S(2)}) %collective-permute-start.33) | collective-permute-done | bytes 159776 | tf_op jit(solution)/shard_map/ppermute | solution.py:72
  305.5 2.5 collective-permute-done.32
  308.0 1.2 fusion.4
  311.1 1.7 copy-done.33
  (168 shorter events, 21.3 us)
Async XLA Ops:
  0.6 23.6 %copy-start.14 = (f32[768,192]{0,1:T(8,128)S(1)}, f32[768,192]{0,1:T(8,128)}, u32[]{:S(2)}) copy-start(f32[768,192]{0,1:T(8,128)} %param.20) | copy-start | bytes 1769476
  2.4 10.2 %collective-permute-start.2 = (bf16[104,768]{1,0:T(8,128)(2,1)S(1)}, bf16[104,768]{1,0:T(8,128)(2,1)S(1)}, u32[]{:S(2)}, u32[]{:S(2)}) collective-permute-start(bf16[104,768]{1,0:T(8,128)(2,1)S(1)} %get-tuple-element.121), channel_id=1, source_target_pairs={{0,24},{1,25},{2,26},{3,27},{4,28},{5,29},{6,30},{7,31},{8,16},{9,... | collective-permute-start | bytes 479240 | tf_op jit(solution)/shard_map/ppermute | solution.py:72
  7.5 13.5 %collective-permute-start.1 = (bf16[104,768]{1,0:T(8,128)(2,1)S(1)}, bf16[104,768]{1,0:T(8,128)(2,1)S(1)}, u32[]{:S(2)}, u32[]{:S(2)}) collective-permute-start(bf16[104,768]{1,0:T(8,128)(2,1)S(1)} %get-tuple-element.121), channel_id=1, source_target_pairs={{0,16},{1,17},{2,18},{3,19},{4,20},{5,21},{6,22},{7,23},{8,24},{9,... | collective-permute-start | bytes 479240 | tf_op jit(solution)/shard_map/ppermute | solution.py:72
  7.5 13.5 %collective-permute-start = (bf16[104,768]{1,0:T(8,128)(2,1)S(1)}, bf16[104,768]{1,0:T(8,128)(2,1)S(1)}, u32[]{:S(2)}, u32[]{:S(2)}) collective-permute-start(bf16[104,768]{1,0:T(8,128)(2,1)S(1)} %get-tuple-element.121), channel_id=1, source_target_pairs={{0,8},{1,9},{2,10},{3,11},{4,12},{5,13},{6,14},{7,15},{8,0},{9,1},... | collective-permute-start | bytes 479240 | tf_op jit(solution)/shard_map/ppermute | solution.py:72
  21.2 35.9 %copy-start = (bf16[4,104,768]{2,1,0:T(8,128)(2,1)}, bf16[4,104,768]{2,1,0:T(8,128)(2,1)S(1)}, u32[]{:S(2)}) copy-start(bf16[4,104,768]{2,1,0:T(8,128)(2,1)S(1)} %pad_maximum_fusion.r_4_.r_7_.r_3_) | copy-start | bytes 1916932
  21.2 17.3 %collective-permute-start.3 = (bf16[4,104,768]{2,1,0:T(8,128)(2,1)S(1)}, bf16[4,104,768]{2,1,0:T(8,128)(2,1)S(1)}, u32[]{:S(2)}, u32[]{:S(2)}) collective-permute-start(bf16[4,104,768]{2,1,0:T(8,128)(2,1)S(1)} %pad_maximum_fusion.r_4_.r_7_.r_3_), channel_id=1, source_target_pairs={{0,2},{1,5},{2,0},{3,7},{4,6},{5,1},{6,4},{7,3},{8,10},{9,13},{10,... | collective-permute-start | bytes 1916936 | tf_op jit(solution)/shard_map/ppermute | solution.py:72
  22.8 21.1 %collective-permute-start.4 = (bf16[4,104,768]{2,1,0:T(8,128)(2,1)S(1)}, bf16[4,104,768]{2,1,0:T(8,128)(2,1)S(1)}, u32[]{:S(2)}, u32[]{:S(2)}) collective-permute-start(bf16[4,104,768]{2,1,0:T(8,128)(2,1)S(1)} %pad_maximum_fusion.r_4_.r_7_.r_3_), channel_id=1, source_target_pairs={{0,4},{1,3},{2,6},{3,1},{4,0},{5,7},{6,2},{7,5},{8,12},{9,11},{10,... | collective-permute-start | bytes 1916936 | tf_op jit(solution)/shard_map/ppermute | solution.py:72
  24.3 19.6 %collective-permute-start.6 = (bf16[4,104,768]{2,1,0:T(8,128)(2,1)S(1)}, bf16[4,104,768]{2,1,0:T(8,128)(2,1)S(1)}, u32[]{:S(2)}, u32[]{:S(2)}) collective-permute-start(bf16[4,104,768]{2,1,0:T(8,128)(2,1)S(1)} %pad_maximum_fusion.r_4_.r_7_.r_3_), channel_id=1, source_target_pairs={{0,1},{1,0},{2,3},{3,2},{4,5},{5,4},{6,7},{7,6},{8,9},{9,8},{10,11... | collective-permute-start | bytes 1916936 | tf_op jit(solution)/shard_map/ppermute | solution.py:72
  27.4 14.9 %collective-permute-start.11 = (bf16[192,768]{1,0:T(8,128)(2,1)}, bf16[192,768]{1,0:T(8,128)(2,1)S(1)}, u32[]{:S(2)}, u32[]{:S(2)}) collective-permute-start(bf16[192,768]{1,0:T(8,128)(2,1)} %ordered_block.1.r_0_), channel_id=1, source_target_pairs={{0,8},{1,9},{2,10},{3,11},{4,12},{5,13},{6,14},{7,15},{8,0},{9,1},... | collective-permute-start | bytes 884744 | tf_op jit(solution)/shard_map/ppermute | solution.py:72
  28.2 17.4 %collective-permute-start.12 = (bf16[192,768]{1,0:T(8,128)(2,1)}, bf16[192,768]{1,0:T(8,128)(2,1)S(1)}, u32[]{:S(2)}, u32[]{:S(2)}) collective-permute-start(bf16[192,768]{1,0:T(8,128)(2,1)} %ordered_block.1.r_0_), channel_id=1, source_target_pairs={{0,16},{1,17},{2,18},{3,19},{4,20},{5,21},{6,22},{7,23},{8,24},{9,... | collective-permute-start | bytes 884744 | tf_op jit(solution)/shard_map/ppermute | solution.py:72
  38.5 24.7 %copy-start.2 = (bf16[4,104,768]{2,1,0:T(8,128)(2,1)}, bf16[4,104,768]{2,1,0:T(8,128)(2,1)S(1)}, u32[]{:S(2)}) copy-start(bf16[4,104,768]{2,1,0:T(8,128)(2,1)S(1)} %collective-permute-done.3.r_5_.r_8_.r_4_) | copy-start | bytes 1916932
  38.5 14.7 %collective-permute-start.5 = (bf16[4,104,768]{2,1,0:T(8,128)(2,1)S(1)}, bf16[4,104,768]{2,1,0:T(8,128)(2,1)S(1)}, u32[]{:S(2)}, u32[]{:S(2)}) collective-permute-start(bf16[4,104,768]{2,1,0:T(8,128)(2,1)S(1)} %collective-permute-done.3.r_5_.r_8_.r_4_), channel_id=1, source_target_pairs={{0,4},{1,3},{2,6},{3,1},{4,0},{5,7},{6,2},{7,5},{8,12},{9,11},{10,... | collective-permute-start | bytes 1916936 | tf_op jit(solution)/shard_map/ppermute | solution.py:72
  42.4 10.8 %copy-start.26 = (bf16[192,768]{1,0:T(8,128)(2,1)}, bf16[192,768]{1,0:T(8,128)(2,1)S(1)}, u32[]{:S(2)}) copy-start(bf16[192,768]{1,0:T(8,128)(2,1)S(1)} %collective-permute-done.11.r_1_) | copy-start | bytes 884740
  42.4 10.8 %collective-permute-start.13 = (bf16[192,768]{1,0:T(8,128)(2,1)}, bf16[192,768]{1,0:T(8,128)(2,1)S(1)}, u32[]{:S(2)}, u32[]{:S(2)}) collective-permute-start(bf16[192,768]{1,0:T(8,128)(2,1)} %ordered_block.1.r_0_), channel_id=1, source_target_pairs={{0,24},{1,25},{2,26},{3,27},{4,28},{5,29},{6,30},{7,31},{8,16},{9,... | collective-permute-start | bytes 884744 | tf_op jit(solution)/shard_map/ppermute | solution.py:72
  43.9 19.4 %copy-start.3 = (bf16[4,104,768]{2,1,0:T(8,128)(2,1)}, bf16[4,104,768]{2,1,0:T(8,128)(2,1)S(1)}, u32[]{:S(2)}) copy-start(bf16[4,104,768]{2,1,0:T(8,128)(2,1)S(1)} %collective-permute-done.4.r_6_.r_9_.r_5_) | copy-start | bytes 1916932
  43.9 15.1 %collective-permute-start.7 = (bf16[4,104,768]{2,1,0:T(8,128)(2,1)S(1)}, bf16[4,104,768]{2,1,0:T(8,128)(2,1)S(1)}, u32[]{:S(2)}, u32[]{:S(2)}) collective-permute-start(bf16[4,104,768]{2,1,0:T(8,128)(2,1)S(1)} %collective-permute-done.3.r_5_.r_8_.r_4_), channel_id=1, source_target_pairs={{0,1},{1,0},{2,3},{3,2},{4,5},{5,4},{6,7},{7,6},{8,9},{9,8},{10,11... | collective-permute-start | bytes 1916936 | tf_op jit(solution)/shard_map/ppermute | solution.py:72
  43.9 19.4 %copy-start.4 = (bf16[4,104,768]{2,1,0:T(8,128)(2,1)}, bf16[4,104,768]{2,1,0:T(8,128)(2,1)S(1)}, u32[]{:S(2)}) copy-start(bf16[4,104,768]{2,1,0:T(8,128)(2,1)S(1)} %collective-permute-done.6.r_8_.r_11_.r_7_) | copy-start | bytes 1916932
  43.9 15.1 %collective-permute-start.8 = (bf16[4,104,768]{2,1,0:T(8,128)(2,1)S(1)}, bf16[4,104,768]{2,1,0:T(8,128)(2,1)S(1)}, u32[]{:S(2)}, u32[]{:S(2)}) collective-permute-start(bf16[4,104,768]{2,1,0:T(8,128)(2,1)S(1)} %collective-permute-done.4.r_6_.r_9_.r_5_), channel_id=1, source_target_pairs={{0,1},{1,0},{2,3},{3,2},{4,5},{5,4},{6,7},{7,6},{8,9},{9,8},{10,11... | collective-permute-start | bytes 1916936 | tf_op jit(solution)/shard_map/ppermute | solution.py:72
  45.6 17.6 %collective-permute-start.10 = (bf16[4,256,768]{2,1,0:T(8,128)(2,1)}, bf16[4,256,768]{2,1,0:T(8,128)(2,1)}, u32[]{:S(2)}, u32[]{:S(2)}) collective-permute-start(bf16[4,256,768]{2,1,0:T(8,128)(2,1)} %r_2_.1), channel_id=1, source_target_pairs={{0,1},{1,0},{2,3},{3,2},{4,5},{5,4},{6,7},{7,6},{8,9},{9,8},{10,11... | collective-permute-start | bytes 4718600 | tf_op jit(solution)/shard_map/ppermute | solution.py:72
  57.0 29.1 %collective-permute-start.14 = (bf16[4,192,768]{2,1,0:T(8,128)(2,1)}, bf16[4,192,768]{2,1,0:T(8,128)(2,1)}, u32[]{:S(2)}, u32[]{:S(2)}) collective-permute-start(bf16[4,192,768]{2,1,0:T(8,128)(2,1)} %ordered_stack.1.r_7_), channel_id=1, source_target_pairs={{0,2},{1,5},{2,0},{3,7},{4,6},{5,1},{6,4},{7,3},{8,10},{9,13},{10,... | collective-permute-start | bytes 3538952 | tf_op jit(solution)/shard_map/ppermute | solution.py:72
  57.6 30.8 %collective-permute-start.16 = (bf16[4,192,768]{2,1,0:T(8,128)(2,1)}, bf16[4,192,768]{2,1,0:T(8,128)(2,1)}, u32[]{:S(2)}, u32[]{:S(2)}) collective-permute-start(bf16[4,192,768]{2,1,0:T(8,128)(2,1)} %ordered_stack.1.r_7_), channel_id=1, source_target_pairs={{0,4},{1,3},{2,6},{3,1},{4,0},{5,7},{6,2},{7,5},{8,12},{9,11},{10,... | collective-permute-start | bytes 3538952 | tf_op jit(solution)/shard_map/ppermute | solution.py:72
  58.9 2.4 collective-permute-start.9
  86.2 16.5 %collective-permute-start.17 = (bf16[4,192,768]{2,1,0:T(8,128)(2,1)}, bf16[4,192,768]{2,1,0:T(8,128)(2,1)S(1)}, u32[]{:S(2)}, u32[]{:S(2)}) collective-permute-start(bf16[4,192,768]{2,1,0:T(8,128)(2,1)} %gate.2.r_20_.r_8_), channel_id=1, source_target_pairs={{0,4},{1,3},{2,6},{3,1},{4,0},{5,7},{6,2},{7,5},{8,12},{9,11},{10,... | collective-permute-start | bytes 3538952 | tf_op jit(solution)/shard_map/ppermute | solution.py:72
  87.7 15.9 %collective-permute-start.15 = (bf16[4,256,768]{2,1,0:T(8,128)(2,1)S(1)}, bf16[4,256,768]{2,1,0:T(8,128)(2,1)S(1)}, u32[]{:S(2)}, u32[]{:S(2)}) collective-permute-start(bf16[4,256,768]{2,1,0:T(8,128)(2,1)S(1)} %copy-done.15), channel_id=1, source_target_pairs={{0,1},{1,0},{2,3},{3,2},{4,5},{5,4},{6,7},{7,6},{8,9},{9,8},{10,11... | collective-permute-start | bytes 4718600 | tf_op jit(solution)/shard_map/ppermute | solution.py:72
  87.9 15.8 %collective-permute-start.18 = (bf16[4,192,768]{2,1,0:T(8,128)(2,1)S(1)}, bf16[4,192,768]{2,1,0:T(8,128)(2,1)S(1)}, u32[]{:S(2)}, u32[]{:S(2)}) collective-permute-start(bf16[4,192,768]{2,1,0:T(8,128)(2,1)S(1)} %copy-done.10), channel_id=1, source_target_pairs={{0,1},{1,0},{2,3},{3,2},{4,5},{5,4},{6,7},{7,6},{8,9},{9,8},{10,11... | collective-permute-start | bytes 3538952 | tf_op jit(solution)/shard_map/ppermute | solution.py:72
  88.2 15.5 %collective-permute-start.19 = (bf16[4,192,768]{2,1,0:T(8,128)(2,1)}, bf16[4,192,768]{2,1,0:T(8,128)(2,1)}, u32[]{:S(2)}, u32[]{:S(2)}) collective-permute-start(bf16[4,192,768]{2,1,0:T(8,128)(2,1)} %gate.2.r_20_.r_8_), channel_id=1, source_target_pairs={{0,1},{1,0},{2,3},{3,2},{4,5},{5,4},{6,7},{7,6},{8,9},{9,8},{10,11... | collective-permute-start | bytes 3538952 | tf_op jit(solution)/shard_map/ppermute | solution.py:72
  88.4 15.3 %collective-permute-start.20 = (bf16[4,192,768]{2,1,0:T(8,128)(2,1)}, bf16[4,192,768]{2,1,0:T(8,128)(2,1)}, u32[]{:S(2)}, u32[]{:S(2)}) collective-permute-start(bf16[4,192,768]{2,1,0:T(8,128)(2,1)} %collective-permute-done.16.r_9_), channel_id=1, source_target_pairs={{0,1},{1,0},{2,3},{3,2},{4,5},{5,4},{6,7},{7,6},{8,9},{9,8},{10,11... | collective-permute-start | bytes 3538952 | tf_op jit(solution)/shard_map/ppermute | solution.py:72
  103.6 3.1 collective-permute-start.21
  170.8 8.2 %collective-permute-start.23 = (bf16[16,192,768]{2,1,0:T(8,128)(2,1)}, bf16[16,192,768]{2,1,0:T(8,128)(2,1)S(1)}, u32[]{:S(2)}, u32[]{:S(2)}) collective-permute-start(bf16[16,192,768]{2,1,0:T(8,128)(2,1)} %get-tuple-element.66), channel_id=1, source_target_pairs={{0,1},{1,0},{2,3},{3,2},{4,5},{5,4},{6,7},{7,6},{8,9},{9,8},{10,11... | collective-permute-start | bytes 14155784 | tf_op jit(solution)/shard_map/ppermute | solution.py:72
  179.0 44.9 %copy-start.13 = (bf16[16,192,768]{2,1,0:T(8,128)(2,1)}, bf16[16,192,768]{2,1,0:T(8,128)(2,1)S(1)}, u32[]{:S(2)}) copy-start(bf16[16,192,768]{2,1,0:T(8,128)(2,1)S(1)} %collective-permute-done.23) | copy-start | bytes 14155780
  182.9 17.1 %collective-permute-start.24 = (bf16[4,192,768]{2,1,0:T(8,128)(2,1)S(1)}, bf16[4,192,768]{2,1,0:T(8,128)(2,1)}, u32[]{:S(2)}, u32[]{:S(2)}) collective-permute-start(bf16[4,192,768]{2,1,0:T(8,128)(2,1)S(1)} %get-tuple-element.114.r_7_), channel_id=1, source_target_pairs={{0,4},{1,3},{2,6},{3,1},{4,0},{5,7},{6,2},{7,5},{8,12},{9,11},{10,... | collective-permute-start | bytes 3538952 | tf_op jit(solution)/shard_map/ppermute | solution.py:72
  184.5 34.7 %collective-permute-start.25 = (bf16[4,192,768]{2,1,0:T(8,128)(2,1)S(1)}, bf16[4,192,768]{2,1,0:T(8,128)(2,1)}, u32[]{:S(2)}, u32[]{:S(2)}) collective-permute-start(bf16[4,192,768]{2,1,0:T(8,128)(2,1)S(1)} %get-tuple-element.113.r_8_), channel_id=1, source_target_pairs={{0,4},{1,3},{2,6},{3,1},{4,0},{5,7},{6,2},{7,5},{8,12},{9,11},{10,... | collective-permute-start | bytes 3538952 | tf_op jit(solution)/shard_map/ppermute | solution.py:72
  202.1 21.8 %collective-permute-start.26 = (bf16[4,192,768]{2,1,0:T(8,128)(2,1)S(1)}, bf16[4,192,768]{2,1,0:T(8,128)(2,1)}, u32[]{:S(2)}, u32[]{:S(2)}) collective-permute-start(bf16[4,192,768]{2,1,0:T(8,128)(2,1)S(1)} %add_convert_fusion.r_8_), channel_id=1, source_target_pairs={{0,2},{1,5},{2,0},{3,7},{4,6},{5,1},{6,4},{7,3},{8,10},{9,13},{10,... | collective-permute-start | bytes 3538952 | tf_op jit(solution)/shard_map/ppermute | solution.py:72
  237.1 5.2 %collective-permute-start.28 = (bf16[16,104,768]{2,1,0:T(8,128)(2,1)}, bf16[16,104,768]{2,1,0:T(8,128)(2,1)S(1)}, u32[]{:S(2)}, u32[]{:S(2)}) collective-permute-start(bf16[16,104,768]{2,1,0:T(8,128)(2,1)} %get-tuple-element.81), channel_id=1, source_target_pairs={{0,1},{1,0},{2,3},{3,2},{4,5},{5,4},{6,7},{7,6},{8,9},{9,8},{10,11... | collective-permute-start | bytes 7667720 | tf_op jit(solution)/shard_map/ppermute | solution.py:72
  244.8 14.4 %collective-permute-start.30 = (bf16[4,104,768]{2,1,0:T(8,128)(2,1)S(1)}, bf16[4,104,768]{2,1,0:T(8,128)(2,1)S(1)}, u32[]{:S(2)}, u32[]{:S(2)}) collective-permute-start(bf16[4,104,768]{2,1,0:T(8,128)(2,1)S(1)} %get-tuple-element.119), channel_id=1, source_target_pairs={{0,4},{1,3},{2,6},{3,1},{4,0},{5,7},{6,2},{7,5},{8,12},{9,11},{10,... | collective-permute-start | bytes 1916936 | tf_op jit(solution)/shard_map/ppermute | solution.py:72
  246.2 22.6 %collective-permute-start.22 = (bf16[2,256,768]{2,1,0:T(8,128)(2,1)}, bf16[2,256,768]{2,1,0:T(8,128)(2,1)}, u32[]{:S(2)}, u32[]{:S(2)}) collective-permute-start(bf16[2,256,768]{2,1,0:T(8,128)(2,1)} %get-tuple-element.60), channel_id=1, source_target_pairs={{0,1},{1,0},{2,3},{3,2},{4,5},{5,4},{6,7},{7,6},{8,9},{9,8},{10,11... | collective-permute-start | bytes 2359304 | tf_op jit(solution)/shard_map/ppermute | solution.py:72
  246.3 22.5 %collective-permute-start.29 = (bf16[4,104,768]{2,1,0:T(8,128)(2,1)}, bf16[4,104,768]{2,1,0:T(8,128)(2,1)}, u32[]{:S(2)}, u32[]{:S(2)}) collective-permute-start(bf16[4,104,768]{2,1,0:T(8,128)(2,1)} %get-tuple-element.118), channel_id=1, source_target_pairs={{0,4},{1,3},{2,6},{3,1},{4,0},{5,7},{6,2},{7,5},{8,12},{9,11},{10,... | collective-permute-start | bytes 1916936 | tf_op jit(solution)/shard_map/ppermute | solution.py:72
  261.3 10.7 %collective-permute-start.31 = (bf16[4,104,768]{2,1,0:T(8,128)(2,1)}, bf16[4,104,768]{2,1,0:T(8,128)(2,1)}, u32[]{:S(2)}, u32[]{:S(2)}) collective-permute-start(bf16[4,104,768]{2,1,0:T(8,128)(2,1)} %add_convert_fusion.3), channel_id=1, source_target_pairs={{0,2},{1,5},{2,0},{3,7},{4,6},{5,1},{6,4},{7,3},{8,10},{9,13},{10,... | collective-permute-start | bytes 1916936 | tf_op jit(solution)/shard_map/ppermute | solution.py:72
  261.9 13.9 %collective-permute-start.37 = (bf16[192,768]{1,0:T(8,128)(2,1)}, bf16[192,768]{1,0:T(8,128)(2,1)S(1)}, u32[]{:S(2)}, u32[]{:S(2)}) collective-permute-start(bf16[192,768]{1,0:T(8,128)(2,1)} %get-tuple-element.110.r_10_), channel_id=1, source_target_pairs={{0,24},{1,25},{2,26},{3,27},{4,28},{5,29},{6,30},{7,31},{8,16},{9,... | collective-permute-start | bytes 884744 | tf_op jit(solution)/shard_map/ppermute | solution.py:72
  264.0 34.7 %collective-permute-start.36 = (bf16[192,768]{1,0:T(8,128)(2,1)}, bf16[192,768]{1,0:T(8,128)(2,1)S(1)}, u32[]{:S(2)}, u32[]{:S(2)}) collective-permute-start(bf16[192,768]{1,0:T(8,128)(2,1)} %get-tuple-element.111.r_9_), channel_id=1, source_target_pairs={{0,16},{1,17},{2,18},{3,19},{4,20},{5,21},{6,22},{7,23},{8,24},{9,... | collective-permute-start | bytes 884744 | tf_op jit(solution)/shard_map/ppermute | solution.py:72
  268.8 29.8 %collective-permute-start.35 = (bf16[192,768]{1,0:T(8,128)(2,1)S(1)}, bf16[192,768]{1,0:T(8,128)(2,1)S(1)}, u32[]{:S(2)}, u32[]{:S(2)}) collective-permute-start(bf16[192,768]{1,0:T(8,128)(2,1)S(1)} %copy-done.19), channel_id=1, source_target_pairs={{0,8},{1,9},{2,10},{3,11},{4,12},{5,13},{6,14},{7,15},{8,0},{9,1},... | collective-permute-start | bytes 884744 | tf_op jit(solution)/shard_map/ppermute | solution.py:72
  268.9 42.1 %collective-permute-start.27 = (f32[2,256,768]{2,1,0:T(8,128)}, f32[2,256,768]{2,1,0:T(8,128)S(1)}, u32[]{:S(2)}, u32[]{:S(2)}) collective-permute-start(f32[2,256,768]{2,1,0:T(8,128)} %get-tuple-element.79), channel_id=1, source_target_pairs={{0,1},{1,0},{2,3},{3,2},{4,5},{5,4},{6,7},{7,6},{8,9},{9,8},{10,11... | collective-permute-start | bytes 4718600 | tf_op jit(solution)/shard_map/ppermute | solution.py:72
  271.0 27.6 %copy-start.22 = (f32[768,192]{0,1:T(8,128)S(1)}, f32[768,192]{0,1:T(8,128)}, u32[]{:S(2)}) copy-start(f32[768,192]{0,1:T(8,128)} %param.22) | copy-start | bytes 1769476
  271.0 27.7 %copy-start.23 = (f32[768,192]{0,1:T(8,128)S(1)}, f32[768,192]{0,1:T(8,128)}, u32[]{:S(2)}) copy-start(f32[768,192]{0,1:T(8,128)} %param.21) | copy-start | bytes 1769476
  273.7 28.2 %collective-permute-start.34 = (bf16[104,768]{1,0:T(8,128)(2,1)S(1)}, bf16[104,768]{1,0:T(8,128)(2,1)S(1)}, u32[]{:S(2)}, u32[]{:S(2)}) collective-permute-start(bf16[104,768]{1,0:T(8,128)(2,1)S(1)} %get-tuple-element.116), channel_id=1, source_target_pairs={{0,24},{1,25},{2,26},{3,27},{4,28},{5,29},{6,30},{7,31},{8,16},{9,... | collective-permute-start | bytes 479240 | tf_op jit(solution)/shard_map/ppermute | solution.py:72
  275.8 29.7 %collective-permute-start.33 = (bf16[104,768]{1,0:T(8,128)(2,1)S(1)}, bf16[104,768]{1,0:T(8,128)(2,1)S(1)}, u32[]{:S(2)}, u32[]{:S(2)}) collective-permute-start(bf16[104,768]{1,0:T(8,128)(2,1)S(1)} %get-tuple-element.117), channel_id=1, source_target_pairs={{0,16},{1,17},{2,18},{3,19},{4,20},{5,21},{6,22},{7,23},{8,24},{9,... | collective-permute-start | bytes 479240 | tf_op jit(solution)/shard_map/ppermute | solution.py:72
  298.6 9.4 %collective-permute-start.32 = (bf16[104,768]{1,0:T(8,128)(2,1)S(1)}, bf16[104,768]{1,0:T(8,128)(2,1)S(1)}, u32[]{:S(2)}, u32[]{:S(2)}) collective-permute-start(bf16[104,768]{1,0:T(8,128)(2,1)S(1)} %get-tuple-element.115), channel_id=1, source_target_pairs={{0,8},{1,9},{2,10},{3,11},{4,12},{5,13},{6,14},{7,15},{8,0},{9,1},... | collective-permute-start | bytes 479240 | tf_op jit(solution)/shard_map/ppermute | solution.py:72
  298.7 12.3 %copy-start.32 = (f32[4,256,768]{2,1,0:T(8,128)S(1)}, f32[4,256,768]{2,1,0:T(8,128)}, u32[]{:S(2)}) copy-start(f32[4,256,768]{2,1,0:T(8,128)} %get-tuple-element.78) | copy-start | bytes 9437188
  (26 other events, 114.0 us)
